TPU v7x, 256 devices: a whole 4x4x8 slice. The times are simulated.
256 devices in a mesh: row: 8 (over y, core), col: 32 (over x, z).
Axes of the slice: x: 4, y: 4, z: 8, core: 2. Of those that a mesh axis runs over, the one named last changes fastest.
Arguments:
- outside: bfloat16 [4096, 16384], P('row', 'col'), may hold values from 0.0099 to 17.5
- inside_head: bfloat16 [4096, 16384], P('row', 'col'), may hold values from 0.0099 to 17.5
- inside_tail: bfloat16 [4096, 16384], P('row', 'col'), may hold values from 0.0099 to 17.5
- inside_pair: float32 [512, 16384], P(None, 'col'), may hold values from 0.4 to 1.6
- seq_head: int32 [1, 16384], P(None, 'col'), may hold values from 0 to 3
- seq_tail: int32 [1, 16384], P(None, 'col'), may hold values from 0 to 3
- pair_mask: int32 [4, 128], P(None, 'col'), may hold values 0 or 1
- split_weight: float32 [4], replicated, may hold values from 0.5 to 2
- pair_weight: float32 [4, 4], replicated, may hold values from 0.5 to 2
- span_blocks: int32 [1], replicated, may hold values from 32 to 255
- partition: float32 [1], replicated, may hold values from 1 to 3
Outputs:
- outside_out: float32 [4096, 16384], P('row', 'col')
- prob_out: float32 [4096, 16384], P('row', 'col')
All inputs are finite; a program needn't handle non-finite values. No bound on the sum of `pair_mask` on one device may be relied on, other than what follows from the above.
Results may differ from a plain program's by a relative error of at most 0.0003.
Values may be sent and summed in bfloat16 or wider, within the bound.
A program may use at most 64 MiB of HBM per device.

v0:
```python
import jax
import jax.numpy as jnp
from jax import lax
from jax.sharding import PartitionSpec as P

precise = lax.Precision.HIGHEST


def passed_along(x, axis, by):
    length = lax.axis_size(axis)
    return lax.ppermute(x, axis, [(i, (i + by) % length) for i in range(length)])


def finish(
    right_sum,
    left_sum,
    head_codes,
    tail_codes,
    mask_rows,
    pair_rows,
    split_weight,
    pair_weight,
    span_blocks,
    partition,
    owner_factor,
):
    cycles, tile_size = head_codes.shape
    repeat = tile_size // mask_rows.shape[1]
    allowed = jnp.repeat(
        jnp.repeat(mask_rows.astype(jnp.float32), repeat, axis=0), repeat, axis=1
    ).reshape(cycles, tile_size, tile_size)
    letters = jnp.arange(4, dtype=jnp.int32)
    head_hot = (head_codes[:, :, None] == letters[None, None, :]).astype(jnp.float32)
    tail_hot = (tail_codes[:, :, None] == letters[None, None, :]).astype(jnp.float32)
    head_weight = jnp.einsum("mak,k->ma", head_hot, split_weight, precision=precise)
    tail_weight = jnp.einsum("mak,k->ma", tail_hot, split_weight, precision=precise)
    outside_diag = (
        owner_factor
        * allowed
        * (right_sum * tail_weight[:, None, :] + head_weight[:, :, None] * left_sum)
        / tile_size
    )
    pair_table = jnp.einsum("mak,kl,mbl->mab", head_hot, pair_weight, tail_hot, precision=precise)
    positions = jnp.arange(tile_size, dtype=jnp.float32)
    span_nt = (
        tile_size * span_blocks[0].astype(jnp.float32) + positions[None, :] - positions[:, None]
    )
    penalty = jnp.sqrt(64.0 * tile_size / span_nt)
    pair_prob = (
        pair_rows.reshape(cycles, tile_size, tile_size)
        * outside_diag
        * pair_table
        * penalty[None, :, :]
        / partition[0]
    )
    return (
        outside_diag.reshape(cycles * tile_size, tile_size),
        pair_prob.reshape(cycles * tile_size, tile_size),
    )


def as_tiles(array):
    return array.reshape(-1, array.shape[1], array.shape[1])


def move_later(stack):
    return jnp.concatenate([jnp.zeros_like(stack), stack[:-1]], axis=0)


def per_device(
    outside,
    inside_head,
    inside_tail,
    inside_pair,
    seq_head,
    seq_tail,
    pair_mask,
    split_weight,
    pair_weight,
    span_blocks,
    partition,
):
    row_count = lax.axis_size("row")
    row_id = lax.axis_index("row")
    col_id = lax.axis_index("col")
    out_tiles = as_tiles(outside)
    right_sum = jnp.zeros(out_tiles.shape, jnp.float32)
    left_sum = jnp.zeros(out_tiles.shape, jnp.float32)
    for distance in range(1, row_count + 1):
        far_out, far_tail = passed_along((outside, inside_tail), "col", -distance)
        right_sum = right_sum + jnp.einsum(
            "mac,mbc->mab",
            as_tiles(far_out),
            as_tiles(far_tail),
            preferred_element_type=jnp.float32,
        )
    for distance in range(1, row_count + 1):
        if distance < row_count:
            up_head, up_out = passed_along((inside_head, outside), "row", distance)
        else:
            up_head, up_out = (inside_head, outside)
        term = jnp.einsum(
            "mca,mcb->mab", as_tiles(up_head), as_tiles(up_out), preferred_element_type=jnp.float32
        )
        left_sum = left_sum + jnp.where(col_id < distance, move_later(term), term)
    owner_factor = (row_id == col_id % row_count).astype(jnp.float32)
    return finish(
        right_sum,
        left_sum,
        seq_head,
        seq_tail,
        pair_mask,
        inside_pair,
        split_weight,
        pair_weight,
        span_blocks,
        partition,
        owner_factor,
    )


def solution(mesh):
    placed = (
        P("row", "col"),
        P("row", "col"),
        P("row", "col"),
        P(None, "col"),
        P(None, "col"),
        P(None, "col"),
        P(None, "col"),
        P(),
        P(),
        P(),
        P(),
    )
    return jax.shard_map(
        per_device,
        mesh=mesh,
        in_specs=placed,
        out_specs=(P("row", "col"), P("row", "col")),
        check_vma=False,
    )
```

profile of v0, /device:TPU:6, one launch (start us, length us, event | category | flops | bytes accessed | tf_op | source)
XLA Modules:
  0.0 374.5 jit_solution(14327116209452113388)
XLA Ops:
  0.6 6.6 %collective-permute-start.2 = (bf16[512,512]{1,0:T(8,128)(2,1)}, bf16[512,512]{1,0:T(8,128)(2,1)S(1)}, u32[]{:S(2)}, u32[]{:S(2)}) collective-permute-start(bf16[512,512]{1,0:T(8,128)(2,1)} %param.11), channel_id=1, source_target_pairs={{0,30},{1,31},{2,0},{3,1},{4,2},{5,3},{6,4},{7,5},{8,6},{9,7},{10,... | collective-permute-start | bytes 1572872 | tf_op jit(solution)/shard_map/ppermute | solution.py:11
  8.7 5.0 %collective-permute-start.5 = (bf16[512,512]{1,0:T(8,128)(2,1)}, bf16[512,512]{1,0:T(8,128)(2,1)S(1)}, u32[]{:S(2)}, u32[]{:S(2)}) collective-permute-start(bf16[512,512]{1,0:T(8,128)(2,1)} %param.13), channel_id=1, source_target_pairs={{0,29},{1,30},{2,31},{3,0},{4,1},{5,2},{6,3},{7,4},{8,5},{9,6},{10... | collective-permute-start | bytes 1572872 | tf_op jit(solution)/shard_map/ppermute | solution.py:11
  20.8 9.5 %collective-permute-done.2 = bf16[512,512]{1,0:T(8,128)(2,1)S(1)} collective-permute-done((bf16[512,512]{1,0:T(8,128)(2,1)}, bf16[512,512]{1,0:T(8,128)(2,1)S(1)}, u32[]{:S(2)}, u32[]{:S(2)}) %collective-permute-start.2) | collective-permute-done | bytes 524320 | tf_op jit(solution)/shard_map/ppermute | solution.py:11
  30.3 11.6 %collective-permute-start.6 = (bf16[512,512]{1,0:T(8,128)(2,1)}, bf16[512,512]{1,0:T(8,128)(2,1)S(1)}, u32[]{:S(2)}, u32[]{:S(2)}) collective-permute-start(bf16[512,512]{1,0:T(8,128)(2,1)} %param.11), channel_id=1, source_target_pairs={{0,28},{1,29},{2,30},{3,31},{4,0},{5,1},{6,2},{7,3},{8,4},{9,5},{1... | collective-permute-start | bytes 1572872 | tf_op jit(solution)/shard_map/ppermute | solution.py:11
  41.9 44.8 %collective-permute-done.3 = bf16[512,512]{1,0:T(8,128)(2,1)S(1)} collective-permute-done((bf16[512,512]{1,0:T(8,128)(2,1)}, bf16[512,512]{1,0:T(8,128)(2,1)S(1)}, u32[]{:S(2)}, u32[]{:S(2)}) %collective-permute-start.3) | collective-permute-done | bytes 524320 | tf_op jit(solution)/shard_map/ppermute | solution.py:11
  86.7 10.9 %collective-permute-start.7 = (bf16[512,512]{1,0:T(8,128)(2,1)}, bf16[512,512]{1,0:T(8,128)(2,1)S(1)}, u32[]{:S(2)}, u32[]{:S(2)}) collective-permute-start(bf16[512,512]{1,0:T(8,128)(2,1)} %param.13), channel_id=1, source_target_pairs={{0,28},{1,29},{2,30},{3,31},{4,0},{5,1},{6,2},{7,3},{8,4},{9,5},{1... | collective-permute-start | bytes 1572872 | tf_op jit(solution)/shard_map/ppermute | solution.py:11
  100.4 28.5 %collective-permute-done.5 = bf16[512,512]{1,0:T(8,128)(2,1)S(1)} collective-permute-done((bf16[512,512]{1,0:T(8,128)(2,1)}, bf16[512,512]{1,0:T(8,128)(2,1)S(1)}, u32[]{:S(2)}, u32[]{:S(2)}) %collective-permute-start.5) | collective-permute-done | bytes 524320 | tf_op jit(solution)/shard_map/ppermute | solution.py:11
  129.0 17.6 %collective-permute-start.9 = (bf16[512,512]{1,0:T(8,128)(2,1)S(1)}, bf16[512,512]{1,0:T(8,128)(2,1)S(1)}, u32[]{:S(2)}, u32[]{:S(2)}) collective-permute-start(bf16[512,512]{1,0:T(8,128)(2,1)S(1)} %copy-done.7), channel_id=1, source_target_pairs={{0,27},{1,28},{2,29},{3,30},{4,31},{5,0},{6,1},{7,2},{8,3},{9,4},{... | collective-permute-start | bytes 1572872 | tf_op jit(solution)/shard_map/ppermute | solution.py:11
  147.1 21.6 %collective-permute-start.10 = (bf16[512,512]{1,0:T(8,128)(2,1)S(1)}, bf16[512,512]{1,0:T(8,128)(2,1)S(1)}, u32[]{:S(2)}, u32[]{:S(2)}) collective-permute-start(bf16[512,512]{1,0:T(8,128)(2,1)S(1)} %copy-done.6), channel_id=1, source_target_pairs={{0,26},{1,27},{2,28},{3,29},{4,30},{5,31},{6,0},{7,1},{8,2},{9,3},... | collective-permute-start | bytes 1572872 | tf_op jit(solution)/shard_map/ppermute | solution.py:11
  169.2 10.4 %collective-permute-done.8 = bf16[512,512]{1,0:T(8,128)(2,1)S(1)} collective-permute-done((bf16[512,512]{1,0:T(8,128)(2,1)S(1)}, bf16[512,512]{1,0:T(8,128)(2,1)S(1)}, u32[]{:S(2)}, u32[]{:S(2)}) %collective-permute-start.8) | collective-permute-done | bytes 524320 | tf_op jit(solution)/shard_map/ppermute | solution.py:11
  179.6 32.8 %collective-permute-done.9 = bf16[512,512]{1,0:T(8,128)(2,1)S(1)} collective-permute-done((bf16[512,512]{1,0:T(8,128)(2,1)S(1)}, bf16[512,512]{1,0:T(8,128)(2,1)S(1)}, u32[]{:S(2)}, u32[]{:S(2)}) %collective-permute-start.9) | collective-permute-done | bytes 524320 | tf_op jit(solution)/shard_map/ppermute | solution.py:11
  213.0 18.4 %collective-permute-done.11 = bf16[512,512]{1,0:T(8,128)(2,1)S(1)} collective-permute-done((bf16[512,512]{1,0:T(8,128)(2,1)S(1)}, bf16[512,512]{1,0:T(8,128)(2,1)S(1)}, u32[]{:S(2)}, u32[]{:S(2)}) %collective-permute-start.11) | collective-permute-done | bytes 524320 | tf_op jit(solution)/shard_map/ppermute | solution.py:11
  236.1 6.6 %collective-permute-done.12 = bf16[512,512]{1,0:T(8,128)(2,1)S(1)} collective-permute-done((bf16[512,512]{1,0:T(8,128)(2,1)S(1)}, bf16[512,512]{1,0:T(8,128)(2,1)S(1)}, u32[]{:S(2)}, u32[]{:S(2)}) %collective-permute-start.12) | collective-permute-done | bytes 524320 | tf_op jit(solution)/shard_map/ppermute | solution.py:11
  242.7 8.6 %collective-permute-done.13 = bf16[512,512]{1,0:T(8,128)(2,1)S(1)} collective-permute-done((bf16[512,512]{1,0:T(8,128)(2,1)S(1)}, bf16[512,512]{1,0:T(8,128)(2,1)S(1)}, u32[]{:S(2)}, u32[]{:S(2)}) %collective-permute-start.13) | collective-permute-done | bytes 524320 | tf_op jit(solution)/shard_map/ppermute | solution.py:11
  261.4 5.3 %collective-permute-done.26 = bf16[512,512]{1,0:T(8,128)(2,1)S(1)} collective-permute-done((bf16[512,512]{1,0:T(8,128)(2,1)S(1)}, bf16[512,512]{1,0:T(8,128)(2,1)S(1)}, u32[]{:S(2)}, u32[]{:S(2)}) %collective-permute-start.26) | collective-permute-done | bytes 524320 | tf_op jit(solution)/shard_map/ppermute | solution.py:11
  269.4 9.6 %collective-permute-done.27 = bf16[512,512]{1,0:T(8,128)(2,1)S(1)} collective-permute-done((bf16[512,512]{1,0:T(8,128)(2,1)S(1)}, bf16[512,512]{1,0:T(8,128)(2,1)S(1)}, u32[]{:S(2)}, u32[]{:S(2)}) %collective-permute-start.27) | collective-permute-done | bytes 524320 | tf_op jit(solution)/shard_map/ppermute | solution.py:11
  284.4 6.3 %collective-permute-start.21 = (bf16[512,512]{1,0:T(8,128)(2,1)S(1)}, bf16[512,512]{1,0:T(8,128)(2,1)S(1)}, u32[]{:S(2)}, u32[]{:S(2)}) collective-permute-start(bf16[512,512]{1,0:T(8,128)(2,1)S(1)} %copy-done.6), channel_id=1, source_target_pairs={{0,96},{32,128},{64,160},{96,192},{128,224},{160,0},{192,32},{224,... | collective-permute-start | bytes 1572872 | tf_op jit(solution)/shard_map/ppermute | solution.py:11
  290.7 4.9 %collective-permute-done.25 = bf16[512,512]{1,0:T(8,128)(2,1)S(1)} collective-permute-done((bf16[512,512]{1,0:T(8,128)(2,1)S(1)}, bf16[512,512]{1,0:T(8,128)(2,1)S(1)}, u32[]{:S(2)}, u32[]{:S(2)}) %collective-permute-start.25) | collective-permute-done | bytes 524320 | tf_op jit(solution)/shard_map/ppermute | solution.py:11
  300.0 13.8 %collective-permute-start.19 = (bf16[512,512]{1,0:T(8,128)(2,1)S(1)}, bf16[512,512]{1,0:T(8,128)(2,1)S(1)}, u32[]{:S(2)}, u32[]{:S(2)}) collective-permute-start(bf16[512,512]{1,0:T(8,128)(2,1)S(1)} %copy-done.6), channel_id=1, source_target_pairs={{0,64},{32,96},{64,128},{96,160},{128,192},{160,224},{192,0},{224,... | collective-permute-start | bytes 1572872 | tf_op jit(solution)/shard_map/ppermute | solution.py:11
  313.8 19.0 %collective-permute-start.16 = (bf16[512,512]{1,0:T(8,128)(2,1)S(1)}, bf16[512,512]{1,0:T(8,128)(2,1)S(1)}, u32[]{:S(2)}, u32[]{:S(2)}) collective-permute-start(bf16[512,512]{1,0:T(8,128)(2,1)S(1)} %copy-done.5), channel_id=1, source_target_pairs={{0,32},{32,64},{64,96},{96,128},{128,160},{160,192},{192,224},{224... | collective-permute-start | bytes 1572872 | tf_op jit(solution)/shard_map/ppermute | solution.py:11
  333.2 5.1 %collective-permute-start.17 = (bf16[512,512]{1,0:T(8,128)(2,1)S(1)}, bf16[512,512]{1,0:T(8,128)(2,1)S(1)}, u32[]{:S(2)}, u32[]{:S(2)}) collective-permute-start(bf16[512,512]{1,0:T(8,128)(2,1)S(1)} %copy-done.6), channel_id=1, source_target_pairs={{0,32},{32,64},{64,96},{96,128},{128,160},{160,192},{192,224},{224... | collective-permute-start | bytes 1572872 | tf_op jit(solution)/shard_map/ppermute | solution.py:11
  338.3 8.3 %collective-permute-start = (bf16[512,512]{1,0:T(8,128)(2,1)S(1)}, bf16[512,512]{1,0:T(8,128)(2,1)S(1)}, u32[]{:S(2)}, u32[]{:S(2)}) collective-permute-start(bf16[512,512]{1,0:T(8,128)(2,1)S(1)} %copy-done.6), channel_id=1, source_target_pairs={{0,31},{1,0},{2,1},{3,2},{4,3},{5,4},{6,5},{7,6},{8,7},{9,8},{10,9... | collective-permute-start | bytes 1572872 | tf_op jit(solution)/shard_map/ppermute | solution.py:11
  348.5 8.3 %collective-permute-start.1 = (bf16[512,512]{1,0:T(8,128)(2,1)S(1)}, bf16[512,512]{1,0:T(8,128)(2,1)S(1)}, u32[]{:S(2)}, u32[]{:S(2)}) collective-permute-start(bf16[512,512]{1,0:T(8,128)(2,1)S(1)} %copy-done.7), channel_id=1, source_target_pairs={{0,31},{1,0},{2,1},{3,2},{4,3},{5,4},{6,5},{7,6},{8,7},{9,8},{10,9... | collective-permute-start | bytes 1572872 | tf_op jit(solution)/shard_map/ppermute | solution.py:11
  364.0 5.6 %collective-permute-done.17 = bf16[512,512]{1,0:T(8,128)(2,1)S(1)} collective-permute-done((bf16[512,512]{1,0:T(8,128)(2,1)S(1)}, bf16[512,512]{1,0:T(8,128)(2,1)S(1)}, u32[]{:S(2)}, u32[]{:S(2)}) %collective-permute-start.17) | collective-permute-done | bytes 524320 | tf_op jit(solution)/shard_map/ppermute | solution.py:11
  (80 shorter events, 53.1 us)
Async XLA Ops:
  0.6 29.7 %collective-permute-start.2 = (bf16[512,512]{1,0:T(8,128)(2,1)}, bf16[512,512]{1,0:T(8,128)(2,1)S(1)}, u32[]{:S(2)}, u32[]{:S(2)}) collective-permute-start(bf16[512,512]{1,0:T(8,128)(2,1)} %param.11), channel_id=1, source_target_pairs={{0,30},{1,31},{2,0},{3,1},{4,2},{5,3},{6,4},{7,5},{8,6},{9,7},{10,... | collective-permute-start | bytes 1572872 | tf_op jit(solution)/shard_map/ppermute | solution.py:11
  7.3 90.7 %collective-permute-start.4 = (bf16[512,512]{1,0:T(8,128)(2,1)}, bf16[512,512]{1,0:T(8,128)(2,1)S(1)}, u32[]{:S(2)}, u32[]{:S(2)}) collective-permute-start(bf16[512,512]{1,0:T(8,128)(2,1)} %param.11), channel_id=1, source_target_pairs={{0,29},{1,30},{2,31},{3,0},{4,1},{5,2},{6,3},{7,4},{8,5},{9,6},{10... | collective-permute-start | bytes 1572872 | tf_op jit(solution)/shard_map/ppermute | solution.py:11
  8.3 78.4 %collective-permute-start.3 = (bf16[512,512]{1,0:T(8,128)(2,1)}, bf16[512,512]{1,0:T(8,128)(2,1)S(1)}, u32[]{:S(2)}, u32[]{:S(2)}) collective-permute-start(bf16[512,512]{1,0:T(8,128)(2,1)} %param.13), channel_id=1, source_target_pairs={{0,30},{1,31},{2,0},{3,1},{4,2},{5,3},{6,4},{7,5},{8,6},{9,7},{10,... | collective-permute-start | bytes 1572872 | tf_op jit(solution)/shard_map/ppermute | solution.py:11
  8.7 120.2 %collective-permute-start.5 = (bf16[512,512]{1,0:T(8,128)(2,1)}, bf16[512,512]{1,0:T(8,128)(2,1)S(1)}, u32[]{:S(2)}, u32[]{:S(2)}) collective-permute-start(bf16[512,512]{1,0:T(8,128)(2,1)} %param.13), channel_id=1, source_target_pairs={{0,29},{1,30},{2,31},{3,0},{4,1},{5,2},{6,3},{7,4},{8,5},{9,6},{10... | collective-permute-start | bytes 1572872 | tf_op jit(solution)/shard_map/ppermute | solution.py:11
  13.8 242.4 %collective-permute-start.28 = (bf16[512,512]{1,0:T(8,128)(2,1)}, bf16[512,512]{1,0:T(8,128)(2,1)}, u32[]{:S(2)}, u32[]{:S(2)}) collective-permute-start(bf16[512,512]{1,0:T(8,128)(2,1)} %param.12), channel_id=1, source_target_pairs={{0,224},{32,0},{64,32},{96,64},{128,96},{160,128},{192,160},{224,1... | collective-permute-start | bytes 1572872 | tf_op jit(solution)/shard_map/ppermute | solution.py:11
  30.3 116.8 %collective-permute-start.6 = (bf16[512,512]{1,0:T(8,128)(2,1)}, bf16[512,512]{1,0:T(8,128)(2,1)S(1)}, u32[]{:S(2)}, u32[]{:S(2)}) collective-permute-start(bf16[512,512]{1,0:T(8,128)(2,1)} %param.11), channel_id=1, source_target_pairs={{0,28},{1,29},{2,30},{3,31},{4,0},{5,1},{6,2},{7,3},{8,4},{9,5},{1... | collective-permute-start | bytes 1572872 | tf_op jit(solution)/shard_map/ppermute | solution.py:11
  86.7 82.0 %collective-permute-start.7 = (bf16[512,512]{1,0:T(8,128)(2,1)}, bf16[512,512]{1,0:T(8,128)(2,1)S(1)}, u32[]{:S(2)}, u32[]{:S(2)}) collective-permute-start(bf16[512,512]{1,0:T(8,128)(2,1)} %param.13), channel_id=1, source_target_pairs={{0,28},{1,29},{2,30},{3,31},{4,0},{5,1},{6,2},{7,3},{8,4},{9,5},{1... | collective-permute-start | bytes 1572872 | tf_op jit(solution)/shard_map/ppermute | solution.py:11
  98.0 81.6 %collective-permute-start.8 = (bf16[512,512]{1,0:T(8,128)(2,1)S(1)}, bf16[512,512]{1,0:T(8,128)(2,1)S(1)}, u32[]{:S(2)}, u32[]{:S(2)}) collective-permute-start(bf16[512,512]{1,0:T(8,128)(2,1)S(1)} %copy-done.6), channel_id=1, source_target_pairs={{0,27},{1,28},{2,29},{3,30},{4,31},{5,0},{6,1},{7,2},{8,3},{9,4},{... | collective-permute-start | bytes 1572872 | tf_op jit(solution)/shard_map/ppermute | solution.py:11
  129.0 83.4 %collective-permute-start.9 = (bf16[512,512]{1,0:T(8,128)(2,1)S(1)}, bf16[512,512]{1,0:T(8,128)(2,1)S(1)}, u32[]{:S(2)}, u32[]{:S(2)}) collective-permute-start(bf16[512,512]{1,0:T(8,128)(2,1)S(1)} %copy-done.7), channel_id=1, source_target_pairs={{0,27},{1,28},{2,29},{3,30},{4,31},{5,0},{6,1},{7,2},{8,3},{9,4},{... | collective-permute-start | bytes 1572872 | tf_op jit(solution)/shard_map/ppermute | solution.py:11
  147.1 65.8 %collective-permute-start.10 = (bf16[512,512]{1,0:T(8,128)(2,1)S(1)}, bf16[512,512]{1,0:T(8,128)(2,1)S(1)}, u32[]{:S(2)}, u32[]{:S(2)}) collective-permute-start(bf16[512,512]{1,0:T(8,128)(2,1)S(1)} %copy-done.6), channel_id=1, source_target_pairs={{0,26},{1,27},{2,28},{3,29},{4,30},{5,31},{6,0},{7,1},{8,2},{9,3},... | collective-permute-start | bytes 1572872 | tf_op jit(solution)/shard_map/ppermute | solution.py:11
  168.7 62.7 %collective-permute-start.11 = (bf16[512,512]{1,0:T(8,128)(2,1)S(1)}, bf16[512,512]{1,0:T(8,128)(2,1)S(1)}, u32[]{:S(2)}, u32[]{:S(2)}) collective-permute-start(bf16[512,512]{1,0:T(8,128)(2,1)S(1)} %copy-done.7), channel_id=1, source_target_pairs={{0,26},{1,27},{2,28},{3,29},{4,30},{5,31},{6,0},{7,1},{8,2},{9,3},... | collective-permute-start | bytes 1572872 | tf_op jit(solution)/shard_map/ppermute | solution.py:11
  179.6 63.1 %collective-permute-start.12 = (bf16[512,512]{1,0:T(8,128)(2,1)S(1)}, bf16[512,512]{1,0:T(8,128)(2,1)S(1)}, u32[]{:S(2)}, u32[]{:S(2)}) collective-permute-start(bf16[512,512]{1,0:T(8,128)(2,1)S(1)} %copy-done.6), channel_id=1, source_target_pairs={{0,25},{1,26},{2,27},{3,28},{4,29},{5,30},{6,31},{7,0},{8,1},{9,2}... | collective-permute-start | bytes 1572872 | tf_op jit(solution)/shard_map/ppermute | solution.py:11
  212.4 38.9 %collective-permute-start.13 = (bf16[512,512]{1,0:T(8,128)(2,1)S(1)}, bf16[512,512]{1,0:T(8,128)(2,1)S(1)}, u32[]{:S(2)}, u32[]{:S(2)}) collective-permute-start(bf16[512,512]{1,0:T(8,128)(2,1)S(1)} %copy-done.7), channel_id=1, source_target_pairs={{0,25},{1,26},{2,27},{3,28},{4,29},{5,30},{6,31},{7,0},{8,1},{9,2}... | collective-permute-start | bytes 1572872 | tf_op jit(solution)/shard_map/ppermute | solution.py:11
  212.9 41.9 %collective-permute-start.14 = (bf16[512,512]{1,0:T(8,128)(2,1)S(1)}, bf16[512,512]{1,0:T(8,128)(2,1)S(1)}, u32[]{:S(2)}, u32[]{:S(2)}) collective-permute-start(bf16[512,512]{1,0:T(8,128)(2,1)S(1)} %copy-done.6), channel_id=1, source_target_pairs={{0,24},{1,25},{2,26},{3,27},{4,28},{5,29},{6,30},{7,31},{8,0},{9,1... | collective-permute-start | bytes 1572872 | tf_op jit(solution)/shard_map/ppermute | solution.py:11
  256.2 39.5 %collective-permute-start.25 = (bf16[512,512]{1,0:T(8,128)(2,1)S(1)}, bf16[512,512]{1,0:T(8,128)(2,1)S(1)}, u32[]{:S(2)}, u32[]{:S(2)}) collective-permute-start(bf16[512,512]{1,0:T(8,128)(2,1)S(1)} %copy-done.6), channel_id=1, source_target_pairs={{0,160},{32,192},{64,224},{96,0},{128,32},{160,64},{192,96},{224,1... | collective-permute-start | bytes 1572872 | tf_op jit(solution)/shard_map/ppermute | solution.py:11
  259.3 40.7 %collective-permute-start.22 = (bf16[512,512]{1,0:T(8,128)(2,1)S(1)}, bf16[512,512]{1,0:T(8,128)(2,1)S(1)}, u32[]{:S(2)}, u32[]{:S(2)}) collective-permute-start(bf16[512,512]{1,0:T(8,128)(2,1)S(1)} %copy-done.5), channel_id=1, source_target_pairs={{0,128},{32,160},{64,192},{96,224},{128,0},{160,32},{192,64},{224,... | collective-permute-start | bytes 1572872 | tf_op jit(solution)/shard_map/ppermute | solution.py:11
  266.8 47.0 %collective-permute-start.23 = (bf16[512,512]{1,0:T(8,128)(2,1)S(1)}, bf16[512,512]{1,0:T(8,128)(2,1)S(1)}, u32[]{:S(2)}, u32[]{:S(2)}) collective-permute-start(bf16[512,512]{1,0:T(8,128)(2,1)S(1)} %copy-done.6), channel_id=1, source_target_pairs={{0,128},{32,160},{64,192},{96,224},{128,0},{160,32},{192,64},{224,... | collective-permute-start | bytes 1572872 | tf_op jit(solution)/shard_map/ppermute | solution.py:11
  279.1 54.1 %collective-permute-start.20 = (bf16[512,512]{1,0:T(8,128)(2,1)S(1)}, bf16[512,512]{1,0:T(8,128)(2,1)S(1)}, u32[]{:S(2)}, u32[]{:S(2)}) collective-permute-start(bf16[512,512]{1,0:T(8,128)(2,1)S(1)} %copy-done.5), channel_id=1, source_target_pairs={{0,96},{32,128},{64,160},{96,192},{128,224},{160,0},{192,32},{224,... | collective-permute-start | bytes 1572872 | tf_op jit(solution)/shard_map/ppermute | solution.py:11
  284.4 53.9 %collective-permute-start.21 = (bf16[512,512]{1,0:T(8,128)(2,1)S(1)}, bf16[512,512]{1,0:T(8,128)(2,1)S(1)}, u32[]{:S(2)}, u32[]{:S(2)}) collective-permute-start(bf16[512,512]{1,0:T(8,128)(2,1)S(1)} %copy-done.6), channel_id=1, source_target_pairs={{0,96},{32,128},{64,160},{96,192},{128,224},{160,0},{192,32},{224,... | collective-permute-start | bytes 1572872 | tf_op jit(solution)/shard_map/ppermute | solution.py:11
  295.6 52.9 %collective-permute-start.18 = (bf16[512,512]{1,0:T(8,128)(2,1)S(1)}, bf16[512,512]{1,0:T(8,128)(2,1)S(1)}, u32[]{:S(2)}, u32[]{:S(2)}) collective-permute-start(bf16[512,512]{1,0:T(8,128)(2,1)S(1)} %copy-done.5), channel_id=1, source_target_pairs={{0,64},{32,96},{64,128},{96,160},{128,192},{160,224},{192,0},{224,... | collective-permute-start | bytes 1572872 | tf_op jit(solution)/shard_map/ppermute | solution.py:11
  300.0 59.8 %collective-permute-start.19 = (bf16[512,512]{1,0:T(8,128)(2,1)S(1)}, bf16[512,512]{1,0:T(8,128)(2,1)S(1)}, u32[]{:S(2)}, u32[]{:S(2)}) collective-permute-start(bf16[512,512]{1,0:T(8,128)(2,1)S(1)} %copy-done.6), channel_id=1, source_target_pairs={{0,64},{32,96},{64,128},{96,160},{128,192},{160,224},{192,0},{224,... | collective-permute-start | bytes 1572872 | tf_op jit(solution)/shard_map/ppermute | solution.py:11
  313.8 50.3 %collective-permute-start.16 = (bf16[512,512]{1,0:T(8,128)(2,1)S(1)}, bf16[512,512]{1,0:T(8,128)(2,1)S(1)}, u32[]{:S(2)}, u32[]{:S(2)}) collective-permute-start(bf16[512,512]{1,0:T(8,128)(2,1)S(1)} %copy-done.5), channel_id=1, source_target_pairs={{0,32},{32,64},{64,96},{96,128},{128,160},{160,192},{192,224},{224... | collective-permute-start | bytes 1572872 | tf_op jit(solution)/shard_map/ppermute | solution.py:11
  333.2 36.4 %collective-permute-start.17 = (bf16[512,512]{1,0:T(8,128)(2,1)S(1)}, bf16[512,512]{1,0:T(8,128)(2,1)S(1)}, u32[]{:S(2)}, u32[]{:S(2)}) collective-permute-start(bf16[512,512]{1,0:T(8,128)(2,1)S(1)} %copy-done.6), channel_id=1, source_target_pairs={{0,32},{32,64},{64,96},{96,128},{128,160},{160,192},{192,224},{224... | collective-permute-start | bytes 1572872 | tf_op jit(solution)/shard_map/ppermute | solution.py:11
  338.3 32.2 %collective-permute-start = (bf16[512,512]{1,0:T(8,128)(2,1)S(1)}, bf16[512,512]{1,0:T(8,128)(2,1)S(1)}, u32[]{:S(2)}, u32[]{:S(2)}) collective-permute-start(bf16[512,512]{1,0:T(8,128)(2,1)S(1)} %copy-done.6), channel_id=1, source_target_pairs={{0,31},{1,0},{2,1},{3,2},{4,3},{5,4},{6,5},{7,6},{8,7},{9,8},{10,9... | collective-permute-start | bytes 1572872 | tf_op jit(solution)/shard_map/ppermute | solution.py:11
  (16 other events, 382.4 us)
where the time goes:
time: 379 us; the launch traced here: 375 us
  waiting for transfers between devices  198 us (52%)
  starting transfers between devices  158 us (42%)
  matrix products  13.5 us (4%)
    ppermute x30, waiting for transfers between devices, passed_along(): lax.ppermute(x, axis, [(i, (i + by) % length) for i in range(length)])  198 us
    ppermute x30, starting transfers between devices, passed_along(): lax.ppermute(x, axis, [(i, (i + by) % length) for i in range(length)])  158 us
  transfers between devices with their start and end apart: 30, of which 16 were waited for; matrix products, arithmetic and copies ran while one was open for 3% of the time, Pallas kernels for 0%

commit v1 on v0

v1 whole, which is shorter than its diff:
```python
import functools
import math

import jax
import jax.numpy as jnp
from jax import lax
from jax.experimental import pallas as pl
from jax.experimental.pallas import tpu as pltpu
from jax.sharding import PartitionSpec as P

MESH = pl.DeviceIdType.MESH
BLK = 512
ROWS = 8
COLS = 32
RIGHT_CHUNK = 32
RIGHT_CHUNKS = BLK // RIGHT_CHUNK
LEFT_CHUNK = 128
LEFT_CHUNKS = BLK // LEFT_CHUNK

LOG_LOW = math.log(BLK * 0.0099**2) - 0.01
LOG_HIGH = math.log(3 * BLK * 17.5**2) + 0.01
LOG_MIDDLE = (LOG_LOW + LOG_HIGH) / 2
LOG_STEP = (LOG_HIGH - LOG_LOW) / 65534


def encode(x):
    code = jnp.round((jnp.log(x) - LOG_MIDDLE) * (1.0 / LOG_STEP))
    return jnp.clip(code, -32767.0, 32767.0).astype(jnp.int32).astype(jnp.int16)


def decode(code):
    return jnp.exp(code.astype(jnp.int32).astype(jnp.float32) * LOG_STEP + LOG_MIDDLE)


def kernel(
    outside,
    inside_head,
    inside_tail,
    inside_pair,
    seq_head_any,
    seq_tail_any,
    pair_mask_any,
    split_weight_any,
    pair_weight_any,
    span_blocks_any,
    partition_any,
    outside_out,
    prob_out,
    out_tile,
    head_tile,
    tail_tile,
    factor,
    seq_head,
    seq_tail,
    pair_mask,
    split_weight,
    pair_weight,
    span_blocks,
    partition,
    right,
    left,
    right_code,
    left_code,
    right_in,
    left_in,
    load_sem,
    right_send,
    right_recv,
    left_send,
    left_recv,
):
    row = lax.axis_index("row")
    col = lax.axis_index("col")
    core = lax.rem(row, 2)
    along = lax.rem(col - 2 * (row // 2) + 32, 8)
    reach = lax.rem(col - row + 31, 8) + 1
    is_owner = reach == 8
    owner_row = lax.rem(col, 8)

    def at_col(c):
        return (row, lax.rem(c + COLS, COLS))

    def at_row(r):
        return (lax.rem(r + ROWS, ROWS), col)

    has_up = (along == 2) | (along == 3) | (along == 6) | (along == 7)
    passes_on = (along >= 3) & (along <= 6)
    next_col = jnp.where(passes_on, jnp.where(along <= 4, col - 1, col + 1), col - reach)
    next_slot = jnp.where(
        passes_on | (along == 2), 0, jnp.where(along == 7, 1, jnp.where(is_owner, 3, 2))
    )

    loads = [
        pltpu.make_async_copy(src, dst, load_sem.at[n])
        for n, (src, dst) in enumerate(
            ((outside, out_tile), (inside_tail, tail_tile), (inside_head, head_tile))
        )
    ]
    for load in loads:
        load.start()

    barrier = pltpu.get_barrier_semaphore()

    @pl.when(has_up)
    def _():
        up = jnp.where(along <= 3, col + 1, col - 1)
        pl.semaphore_signal(barrier, inc=1, device_id=at_col(up), device_id_type=MESH)

    @pl.when(is_owner)
    def _():
        for far in (2 - core, 7 - core, 1 + 6 * core, 8):
            pl.semaphore_signal(barrier, inc=1, device_id=at_col(col + far), device_id_type=MESH)
        for away in range(1, ROWS):
            pl.semaphore_signal(
                barrier, inc=1, device_id=at_row(row + away), device_id_type=MESH
            )

    loads[0].wait()
    loads[1].wait()

    def right_block(n, carry):
        rows = pl.ds(pl.multiple_of(n * 128, 128), 128)
        right[rows, :] = lax.dot_general(
            out_tile[rows, :],
            tail_tile[...],
            (((1,), (1,)), ((), ())),
            preferred_element_type=jnp.float32,
        )
        return carry

    lax.fori_loop(0, 4, right_block, 0)

    pl.semaphore_wait(barrier, jnp.where(is_owner, 1, 2))

    def right_copy(n):
        rows = pl.ds(pl.multiple_of(n * RIGHT_CHUNK, RIGHT_CHUNK), RIGHT_CHUNK)
        return pltpu.make_async_remote_copy(
            src_ref=right_code.at[rows],
            dst_ref=right_in.at[next_slot, rows],
            send_sem=right_send.at[n],
            recv_sem=right_recv.at[next_slot, n],
            device_id=at_col(next_col),
            device_id_type=MESH,
        )

    def right_arrival(slot, n):
        rows = pl.ds(pl.multiple_of(n * RIGHT_CHUNK, RIGHT_CHUNK), RIGHT_CHUNK)
        return pltpu.make_async_remote_copy(
            src_ref=right_code.at[rows],
            dst_ref=right_in.at[slot, rows],
            send_sem=right_send.at[n],
            recv_sem=right_recv.at[slot, n],
            device_id=at_col(next_col),
            device_id_type=MESH,
        )

    @pl.when(jnp.logical_not(has_up))
    def _():
        def step(n, carry):
            rows = pl.ds(pl.multiple_of(n * RIGHT_CHUNK, RIGHT_CHUNK), RIGHT_CHUNK)
            right_code[rows, :] = encode(right[rows, :])
            right_copy(n).start()
            return carry

        lax.fori_loop(0, RIGHT_CHUNKS, step, 0)

    loads[2].wait()

    def left_copy(n):
        rows = pl.ds(pl.multiple_of(n * LEFT_CHUNK, LEFT_CHUNK), LEFT_CHUNK)
        slot = lax.rem(row - owner_row + 7, 8)
        return pltpu.make_async_remote_copy(
            src_ref=left_code.at[rows],
            dst_ref=left_in.at[slot, rows],
            send_sem=left_send.at[n],
            recv_sem=left_recv.at[slot, n],
            device_id=at_row(owner_row),
            device_id_type=MESH,
        )

    for n in range(4):
        rows = slice(n * 128, n * 128 + 128)
        left[rows, :] = lax.dot_general(
            head_tile[:, rows],
            out_tile[...],
            (((0,), (0,)), ((), ())),
            preferred_element_type=jnp.float32,
        )

    @pl.when(jnp.logical_not(is_owner))
    def _():
        def step(n, carry):
            rows = pl.ds(pl.multiple_of(n * LEFT_CHUNK, LEFT_CHUNK), LEFT_CHUNK)
            left_code[rows, :] = encode(left[rows, :])
            left_copy(n).start()
            return carry

        lax.fori_loop(0, LEFT_CHUNKS, step, 0)

    @pl.when(has_up)
    def _():
        def step(n, carry):
            rows = pl.ds(pl.multiple_of(n * RIGHT_CHUNK, RIGHT_CHUNK), RIGHT_CHUNK)
            right_arrival(0, n).wait_recv()
            right_code[rows, :] = encode(right[rows, :] + decode(right_in[0, rows, :]))
            right_copy(n).start()
            return carry

        lax.fori_loop(0, RIGHT_CHUNKS, step, 0)

    @pl.when(jnp.logical_not(is_owner))
    def _():
        outside_out[...] = jnp.zeros((BLK, BLK), jnp.float32)
        prob_out[...] = jnp.zeros((BLK, BLK), jnp.float32)

    @pl.when(is_owner)
    def _():
        owner_loads = [
            pltpu.make_async_copy(src, dst, load_sem.at[3 + n])
            for n, (src, dst) in enumerate(
                (
                    (inside_pair, factor),
                    (seq_head_any, seq_head),
                    (seq_tail_any, seq_tail),
                    (pair_mask_any, pair_mask),
                    (split_weight_any, split_weight),
                    (pair_weight_any, pair_weight),
                    (span_blocks_any, span_blocks),
                    (partition_any, partition),
                )
            )
        ]
        for load in owner_loads:
            load.start()
        for load in owner_loads:
            load.wait()
        head_codes = jnp.transpose(
            jnp.broadcast_to(seq_head[...].astype(jnp.float32), (8, BLK)), (1, 0)
        )[:, :1]
        tail_codes = seq_tail[...]

        def chosen(codes, values):
            picked = jnp.where(codes == 1, values[1], values[0])
            picked = jnp.where(codes == 2, values[2], picked)
            return jnp.where(codes == 3, values[3], picked)

        weights = [split_weight[n] for n in range(4)]
        tail_weight = chosen(tail_codes, weights)
        pair_rows = [chosen(tail_codes, [pair_weight[h, t] for t in range(4)]) for h in range(4)]
        lane = lax.broadcasted_iota(jnp.int32, (1, BLK), 1)
        span_nt = BLK * span_blocks[0].astype(jnp.float32)

        blocks = [slice(n * 128, n * 128 + 128) for n in range(4)]
        for rows in blocks:
            codes = head_codes[rows]
            table = chosen(codes, pair_rows)
            place = lax.broadcasted_iota(jnp.int32, (128, BLK), 0) + rows.start
            across = lax.broadcasted_iota(jnp.int32, (128, BLK), 1)
            span = span_nt + (across - place).astype(jnp.float32)
            penalty = jnp.sqrt(64.0 * BLK / span)
            factor[rows, :] = factor[rows, :] * table * penalty / partition[0]

        def left_arrival(slot, n):
            rows = pl.ds(pl.multiple_of(n * LEFT_CHUNK, LEFT_CHUNK), LEFT_CHUNK)
            return pltpu.make_async_remote_copy(
                src_ref=left_code.at[rows],
                dst_ref=left_in.at[slot, rows],
                send_sem=left_send.at[n],
                recv_sem=left_recv.at[slot, n],
                device_id=at_row(owner_row + 1),
                device_id_type=MESH,
            )

        def counts(r):
            return col >= lax.rem(col - r + 31, 8) + 1

        def right_near(n, carry):
            rows = pl.ds(pl.multiple_of(n * RIGHT_CHUNK, RIGHT_CHUNK), RIGHT_CHUNK)
            right_arrival(2, n).wait_recv()
            right_arrival(3, n).wait_recv()
            right[rows, :] = decode(right_in[2, rows, :]) + decode(right_in[3, rows, :])
            return carry

        def left_add(n, carry):
            rows = pl.ds(pl.multiple_of(n * LEFT_CHUNK, LEFT_CHUNK), LEFT_CHUNK)
            total = jnp.where(counts(row), left[rows, :], 0.0)
            for slot in range(7):
                left_arrival(slot, n).wait_recv()
                total = total + jnp.where(
                    counts(lax.rem(row + slot + 1, ROWS)), decode(left_in[slot, rows, :]), 0.0
                )
            left[rows, :] = total
            return carry

        lax.fori_loop(0, RIGHT_CHUNKS, right_near, 0)
        lax.fori_loop(0, LEFT_CHUNKS, left_add, 0)

        for b, rows in enumerate(blocks):
            codes = head_codes[rows]
            head_weight = chosen(codes, weights)
            allowed = chosen(lane // 128, [pair_mask[b, n].astype(jnp.float32) for n in range(4)])
            for part in range(128 // RIGHT_CHUNK):
                n = b * (128 // RIGHT_CHUNK) + part
                here = slice(n * RIGHT_CHUNK, (n + 1) * RIGHT_CHUNK)
                inner = slice(part * RIGHT_CHUNK, (part + 1) * RIGHT_CHUNK)
                right_arrival(0, n).wait_recv()
                right_arrival(1, n).wait_recv()
                right_sum = right[here, :] + decode(right_in[0, here, :]) + decode(right_in[1, here, :])
                diag = (
                    allowed
                    * (right_sum * tail_weight + head_weight[inner] * left[here, :])
                    * (1.0 / BLK)
                )
                outside_out[here, :] = diag
                prob_out[here, :] = diag * factor[here, :]

    def sent(n, carry):
        right_copy(n).wait_send()
        return carry

    lax.fori_loop(0, RIGHT_CHUNKS, sent, 0)

    @pl.when(jnp.logical_not(is_owner))
    def _():
        for n in range(LEFT_CHUNKS):
            left_copy(n).wait_send()


def per_device(*args):
    vmem = pl.BlockSpec(memory_space=pltpu.VMEM)
    anywhere = pl.BlockSpec(memory_space=pl.ANY)
    tile = jax.ShapeDtypeStruct((BLK, BLK), jnp.float32)
    return pl.pallas_call(
        kernel,
        out_shape=(tile, tile),
        in_specs=[anywhere] * 11,
        out_specs=(vmem, vmem),
        scratch_shapes=[
            pltpu.VMEM((BLK, BLK), jnp.bfloat16),
            pltpu.VMEM((BLK, BLK), jnp.bfloat16),
            pltpu.VMEM((BLK, BLK), jnp.bfloat16),
            pltpu.VMEM((BLK, BLK), jnp.float32),
            pltpu.VMEM((1, BLK), jnp.int32),
            pltpu.VMEM((1, BLK), jnp.int32),
            pltpu.SMEM((4, 4), jnp.int32),
            pltpu.SMEM((4,), jnp.float32),
            pltpu.SMEM((4, 4), jnp.float32),
            pltpu.SMEM((1,), jnp.int32),
            pltpu.SMEM((1,), jnp.float32),
            pltpu.VMEM((BLK, BLK), jnp.float32),
            pltpu.VMEM((BLK, BLK), jnp.float32),
            pltpu.VMEM((BLK, BLK), jnp.int16),
            pltpu.VMEM((BLK, BLK), jnp.int16),
            pltpu.VMEM((4, BLK, BLK), jnp.int16),
            pltpu.VMEM((7, BLK, BLK), jnp.int16),
            pltpu.SemaphoreType.DMA((11,)),
            pltpu.SemaphoreType.DMA((RIGHT_CHUNKS,)),
            pltpu.SemaphoreType.DMA((4, RIGHT_CHUNKS)),
            pltpu.SemaphoreType.DMA((LEFT_CHUNKS,)),
            pltpu.SemaphoreType.DMA((7, LEFT_CHUNKS)),
        ],
        compiler_params=pltpu.CompilerParams(
            collective_id=0, has_side_effects=True, vmem_limit_bytes=62 * 1024 * 1024
        ),
        name="outside_window",
    )(*args)


def solution(mesh):
    placed = (P("row", "col"),) * 3 + (P(None, "col"),) * 4 + (P(),) * 4
    return jax.shard_map(
        per_device,
        mesh=mesh,
        in_specs=placed,
        out_specs=(P("row", "col"), P("row", "col")),
        check_vma=False,
    )
```

time: 379 us -> 42.4 us (0.11); the launches traced: 375 us -> 42.1 us
  waiting for transfers between devices: 198 us -> 0 us
  starting transfers between devices: 158 us -> 0 us
  Pallas kernels: 0 us -> 36.8 us
  matrix products: 13.5 us -> 0 us
    ppermute x30 -> x0, waiting for transfers between devices: 198 us -> none  [passed_along(): lax.ppermute(x, axis, [(i, (i + by) % length) for i in range(length)])]
    ppermute x30 -> x0, starting transfers between devices: 158 us -> none  [passed_along(): lax.ppermute(x, axis, [(i, (i + by) % length) for i in range(length)])]
    pallas_call x0 -> x1, Pallas kernels: none -> 36.8 us  [per_device(): pl.pallas_call(kernel, out_shape=(tile, tile), in_specs=[anywhere] * 11,...]
    dot_general x20 -> x0, matrix products: 13.5 us -> none  [the longest x8 6.33 us: per_device(): jnp.einsum('mca,mcb->mab', as_tiles(up_head), as_tiles(up_out), preferred...]
  transfers between devices with their start and end apart: 30 -> 0, of which waited for: 16 -> 0; matrix products, arithmetic and copies ran while one was open for 3% -> 0% of each run, Pallas kernels for 0% -> 0%
where the time goes in v1:
time: 42.4 us; the launch traced here: 42.1 us
  Pallas kernels  36.8 us (87%)
  local copies, waits for them, and re-layouts  3.32 us (8%)
  between operations  1.94 us (5%)
    pallas_call x1, Pallas kernels, per_device(): pl.pallas_call(kernel, out_shape=(tile, tile), in_specs=[anywhere] * 11,...  36.8 us
    unnamed x4, local copies, waits for them, and re-layouts  3.32 us

profile of v1, /device:TPU:6, one launch (start us, length us, event | category | flops | bytes accessed | tf_op | source)
XLA Modules:
  0.0 42.1 jit_solution(12783913754257293730)
XLA Ops:
  1.9 36.8 %outside_window.1 = (f32[512,512]{1,0:T(8,128)}, f32[512,512]{1,0:T(8,128)}) custom-call(bf16[512,512]{1,0:T(8,128)(2,1)} %outside.1, bf16[512,512]{1,0:T(8,128)(2,1)} %inside_head.1, bf16[512,512]{1,0:T(8,128)(2,1)} %inside_tail.1, f32[512,512]{1,0:T(8,128)} %inside_pair.1, s32[1,512]{1,0:T(1,128)} %seq_head_any.1, s32[1,512]{1,0:T(1,128)} %seq_tail_any.1, ...), custom_call_target="tpu_custom_call" | custom-call | tf_op jit(solution)/shard_map/outside_window/pallas_call | solution.py:333
  38.7 0.0 copy-start
  38.7 2.4 %copy.17 = f32[512,512]{1,0:T(8,128)} copy(f32[512,512]{1,0:T(8,128)} %get-tuple-element.4) | data formatting | bytes 2097152
  41.1 0.0 copy-done
  41.1 1.0 %copy.18 = f32[512,512]{1,0:T(8,128)} copy(f32[512,512]{1,0:T(8,128)S(1)} %copy-done) | data formatting | bytes 2097152
Async XLA Ops:
  38.7 2.4 %copy-start = (f32[512,512]{1,0:T(8,128)S(1)}, f32[512,512]{1,0:T(8,128)}, u32[]{:S(2)}) copy-start(f32[512,512]{1,0:T(8,128)} %get-tuple-element.5) | copy-start | bytes 3145732

commit v2 on v1

--- a/solution.py
+++ b/solution.py
@@ -14,8 +14,11 @@
 COLS = 32
 RIGHT_CHUNK = 32
 RIGHT_CHUNKS = BLK // RIGHT_CHUNK
-LEFT_CHUNK = 128
+AHEAD = 2
+FIRST_ROWS = 128
+LEFT_CHUNK = 64
 LEFT_CHUNKS = BLK // LEFT_CHUNK
+HALF_CHUNKS = LEFT_CHUNKS // 2
 
 LOG_LOW = math.log(BLK * 0.0099**2) - 0.01
 LOG_HIGH = math.log(3 * BLK * 17.5**2) + 0.01
@@ -42,8 +45,8 @@
     pair_mask_any,
     split_weight_any,
     pair_weight_any,
-    span_blocks_any,
-    partition_any,
+    span_blocks,
+    partition,
     outside_out,
     prob_out,
     out_tile,
@@ -55,8 +58,6 @@
     pair_mask,
     split_weight,
     pair_weight,
-    span_blocks,
-    partition,
     right,
     left,
     right_code,
@@ -66,8 +67,10 @@
     load_sem,
     right_send,
     right_recv,
+    share_send,
     left_send,
     left_recv,
+    left_ready,
 ):
     row = lax.axis_index("row")
     col = lax.axis_index("col")
@@ -76,6 +79,9 @@
     reach = lax.rem(col - row + 31, 8) + 1
     is_owner = reach == 8
     owner_row = lax.rem(col, 8)
+    chip_away = lax.rem(row // 2 - owner_row // 2 + 4, 4)
+    at_owner_chip = chip_away == 0
+    sibling = row + 1 - 2 * core
 
     def at_col(c):
         return (row, lax.rem(c + COLS, COLS))
@@ -83,12 +89,21 @@
     def at_row(r):
         return (lax.rem(r + ROWS, ROWS), col)
 
-    has_up = (along == 2) | (along == 3) | (along == 6) | (along == 7)
+    gathers = is_owner & (core == 1)
+    near = (along == 0) & (core == 1)
+    has_up = (along == 2) | (along == 3) | (along == 6) | (along == 7) | gathers
     passes_on = (along >= 3) & (along <= 6)
-    next_col = jnp.where(passes_on, jnp.where(along <= 4, col - 1, col + 1), col - reach)
+    next_col = jnp.where(
+        passes_on | near, jnp.where((along == 3) | (along == 4), col - 1, col + 1), col - reach
+    )
     next_slot = jnp.where(
         passes_on | (along == 2), 0, jnp.where(along == 7, 1, jnp.where(is_owner, 3, 2))
     )
+    up_slot = jnp.where(gathers, 2, 0)
+    far = (along == 4) | (along == 5)
+    middle = (along == 3) | (along == 6)
+    last = (along == 2) | (along == 7)
+    far_col = jnp.where(along == 4, col - 2, col + 2)
 
     loads = [
         pltpu.make_async_copy(src, dst, load_sem.at[n])
@@ -101,36 +116,55 @@
 
     barrier = pltpu.get_barrier_semaphore()
 
+    def announce(device):
+        pl.semaphore_signal(barrier, inc=1, device_id=device, device_id_type=MESH)
+
     @pl.when(has_up)
     def _():
-        up = jnp.where(along <= 3, col + 1, col - 1)
-        pl.semaphore_signal(barrier, inc=1, device_id=at_col(up), device_id_type=MESH)
+        announce(at_col(jnp.where((along == 2) | (along == 3), col + 1, col - 1)))
+
+    @pl.when(last)
+    def _():
+        announce(at_col(jnp.where(along == 2, col + 2, col - 2)))
 
     @pl.when(is_owner)
     def _():
-        for far in (2 - core, 7 - core, 1 + 6 * core, 8):
-            pl.semaphore_signal(barrier, inc=1, device_id=at_col(col + far), device_id_type=MESH)
-        for away in range(1, ROWS):
-            pl.semaphore_signal(
-                barrier, inc=1, device_id=at_row(row + away), device_id_type=MESH
-            )
+        for away in (2 - core, 7 - core, 8):
+            announce(at_col(col + away))
+
+    @pl.when(is_owner & (core == 0))
+    def _():
+        announce(at_col(col + 1))
+
+    @pl.when(jnp.logical_not(at_owner_chip & jnp.logical_not(is_owner)))
+    def _():
+        announce(at_row(sibling))
+
+    @pl.when(jnp.logical_not(at_owner_chip))
+    def _():
+        announce(at_row(owner_row))
 
     loads[0].wait()
     loads[1].wait()
 
-    def right_block(n, carry):
-        rows = pl.ds(pl.multiple_of(n * 128, 128), 128)
+    def right_product(rows):
         right[rows, :] = lax.dot_general(
             out_tile[rows, :],
             tail_tile[...],
             (((1,), (1,)), ((), ())),
             preferred_element_type=jnp.float32,
         )
-        return carry
-
-    lax.fori_loop(0, 4, right_block, 0)
-
-    pl.semaphore_wait(barrier, jnp.where(is_owner, 1, 2))
+
+    right_product(slice(0, FIRST_ROWS))
+
+    pl.semaphore_wait(barrier, jnp.where(is_owner, ROWS - 1, jnp.where(far, 3, 2)))
+
+    @pl.when(is_owner)
+    def _():
+        for away in range(2, ROWS):
+            pl.semaphore_signal(
+                left_ready, inc=1, device_id=at_row(row - core + away), device_id_type=MESH
+            )
 
     def right_copy(n):
         rows = pl.ds(pl.multiple_of(n * RIGHT_CHUNK, RIGHT_CHUNK), RIGHT_CHUNK)
@@ -143,6 +177,17 @@
             device_id_type=MESH,
         )
 
+    def ahead_copy(n):
+        rows = pl.ds(pl.multiple_of(n * RIGHT_CHUNK, RIGHT_CHUNK), RIGHT_CHUNK)
+        return pltpu.make_async_remote_copy(
+            src_ref=right_code.at[rows],
+            dst_ref=right_in.at[1, rows],
+            send_sem=right_send.at[n],
+            recv_sem=right_recv.at[1, n],
+            device_id=at_col(far_col),
+            device_id_type=MESH,
+        )
+
     def right_arrival(slot, n):
         rows = pl.ds(pl.multiple_of(n * RIGHT_CHUNK, RIGHT_CHUNK), RIGHT_CHUNK)
         return pltpu.make_async_remote_copy(
@@ -154,59 +199,121 @@
             device_id_type=MESH,
         )
 
-    @pl.when(jnp.logical_not(has_up))
-    def _():
-        def step(n, carry):
-            rows = pl.ds(pl.multiple_of(n * RIGHT_CHUNK, RIGHT_CHUNK), RIGHT_CHUNK)
-            right_code[rows, :] = encode(right[rows, :])
-            right_copy(n).start()
-            return carry
-
-        lax.fori_loop(0, RIGHT_CHUNKS, step, 0)
+    def code_rows(n):
+        rows = pl.ds(pl.multiple_of(n * RIGHT_CHUNK, RIGHT_CHUNK), RIGHT_CHUNK)
+        right_code[rows, :] = encode(right[rows, :])
+
+    def send_own(n, carry):
+        code_rows(n)
+        right_copy(n).start()
+        return carry
+
+    def send_ahead(n, carry):
+        code_rows(n)
+        ahead_copy(n).start()
+        return carry
+
+    first_chunks = FIRST_ROWS // RIGHT_CHUNK
+
+    @pl.when(far)
+    def _():
+        lax.fori_loop(0, AHEAD, send_ahead, 0)
+
+    starts = jnp.logical_not(has_up)
+    lax.fori_loop(
+        jnp.where(far, AHEAD, 0),
+        jnp.where(starts, first_chunks, jnp.where(middle, AHEAD, 0)),
+        send_own,
+        0,
+    )
+    right_product(slice(FIRST_ROWS, BLK))
+    lax.fori_loop(first_chunks, jnp.where(starts, RIGHT_CHUNKS, first_chunks), send_own, 0)
 
     loads[2].wait()
 
+    left[...] = lax.dot_general(
+        head_tile[...],
+        out_tile[...],
+        (((0,), (0,)), ((), ())),
+        preferred_element_type=jnp.float32,
+    )
+
+    def counts(r):
+        return col >= lax.rem(col - r + 31, 8) + 1
+
+    def left_rows(n):
+        return pl.ds(pl.multiple_of(n * LEFT_CHUNK, LEFT_CHUNK), LEFT_CHUNK)
+
+    def share_copy(n):
+        return pltpu.make_async_remote_copy(
+            src_ref=left_code.at[left_rows(n)],
+            dst_ref=left_in.at[0, left_rows(n)],
+            send_sem=share_send.at[n],
+            recv_sem=left_recv.at[0, n],
+            device_id=at_row(sibling),
+            device_id_type=MESH,
+        )
+
     def left_copy(n):
-        rows = pl.ds(pl.multiple_of(n * LEFT_CHUNK, LEFT_CHUNK), LEFT_CHUNK)
-        slot = lax.rem(row - owner_row + 7, 8)
         return pltpu.make_async_remote_copy(
-            src_ref=left_code.at[rows],
-            dst_ref=left_in.at[slot, rows],
+            src_ref=left_code.at[left_rows(n)],
+            dst_ref=left_in.at[chip_away, left_rows(n)],
             send_sem=left_send.at[n],
-            recv_sem=left_recv.at[slot, n],
+            recv_sem=left_recv.at[chip_away, n],
             device_id=at_row(owner_row),
             device_id_type=MESH,
         )
 
-    for n in range(4):
-        rows = slice(n * 128, n * 128 + 128)
-        left[rows, :] = lax.dot_general(
-            head_tile[:, rows],
-            out_tile[...],
-            (((0,), (0,)), ((), ())),
-            preferred_element_type=jnp.float32,
-        )
-
     @pl.when(jnp.logical_not(is_owner))
     def _():
-        def step(n, carry):
-            rows = pl.ds(pl.multiple_of(n * LEFT_CHUNK, LEFT_CHUNK), LEFT_CHUNK)
-            left_code[rows, :] = encode(left[rows, :])
+        def give(n, carry):
+            left_code[left_rows(n), :] = encode(left[left_rows(n), :])
+            share_copy(n).start()
+            return carry
+
+        first = jnp.where(at_owner_chip, 0, (1 - core) * HALF_CHUNKS)
+        last = jnp.where(at_owner_chip, LEFT_CHUNKS, (2 - core) * HALF_CHUNKS)
+        lax.fori_loop(first, last, give, 0)
+
+    @pl.when(jnp.logical_not(at_owner_chip))
+    def _():
+        mine, theirs = counts(row), counts(sibling)
+        pl.semaphore_wait(left_ready, 1)
+
+        def merge(n, carry):
+            rows = left_rows(n)
+            share_copy(n).wait_recv()
+            total = jnp.where(mine, left[rows, :], 0.0)
+            total = total + jnp.where(theirs, decode(left_in[0, rows, :]), 0.0)
+            left_code[rows, :] = encode(jnp.where(mine | theirs, total, 1.0))
             left_copy(n).start()
             return carry
 
-        lax.fori_loop(0, LEFT_CHUNKS, step, 0)
-
-    @pl.when(has_up)
+        lax.fori_loop(core * HALF_CHUNKS, (core + 1) * HALF_CHUNKS, merge, 0)
+
+    @pl.when(last)
     def _():
         def step(n, carry):
             rows = pl.ds(pl.multiple_of(n * RIGHT_CHUNK, RIGHT_CHUNK), RIGHT_CHUNK)
             right_arrival(0, n).wait_recv()
-            right_code[rows, :] = encode(right[rows, :] + decode(right_in[0, rows, :]))
+            right_arrival(1, n).wait_recv()
+            total = right[rows, :] + decode(right_in[0, rows, :]) + decode(right_in[1, rows, :])
+            right_code[rows, :] = encode(total)
             right_copy(n).start()
             return carry
 
-        lax.fori_loop(0, RIGHT_CHUNKS, step, 0)
+        lax.fori_loop(0, AHEAD, step, 0)
+
+    @pl.when(has_up)
+    def _():
+        def step(n, carry):
+            rows = pl.ds(pl.multiple_of(n * RIGHT_CHUNK, RIGHT_CHUNK), RIGHT_CHUNK)
+            right_arrival(up_slot, n).wait_recv()
+            right_code[rows, :] = encode(right[rows, :] + decode(right_in[up_slot, rows, :]))
+            right_copy(n).start()
+            return carry
+
+        lax.fori_loop(jnp.where(gathers, 0, AHEAD), RIGHT_CHUNKS, step, 0)
 
     @pl.when(jnp.logical_not(is_owner))
     def _():
@@ -225,8 +332,6 @@
                     (pair_mask_any, pair_mask),
                     (split_weight_any, split_weight),
                     (pair_weight_any, pair_weight),
-                    (span_blocks_any, span_blocks),
-                    (partition_any, partition),
                 )
             )
         ]
@@ -261,38 +366,44 @@
             factor[rows, :] = factor[rows, :] * table * penalty / partition[0]
 
         def left_arrival(slot, n):
-            rows = pl.ds(pl.multiple_of(n * LEFT_CHUNK, LEFT_CHUNK), LEFT_CHUNK)
             return pltpu.make_async_remote_copy(
-                src_ref=left_code.at[rows],
-                dst_ref=left_in.at[slot, rows],
+                src_ref=left_code.at[left_rows(n)],
+                dst_ref=left_in.at[slot, left_rows(n)],
                 send_sem=left_send.at[n],
                 recv_sem=left_recv.at[slot, n],
-                device_id=at_row(owner_row + 1),
+                device_id=at_row(sibling),
                 device_id_type=MESH,
             )
 
-        def counts(r):
-            return col >= lax.rem(col - r + 31, 8) + 1
-
         def right_near(n, carry):
             rows = pl.ds(pl.multiple_of(n * RIGHT_CHUNK, RIGHT_CHUNK), RIGHT_CHUNK)
+            right_arrival(3, n).wait_recv()
+            right[rows, :] = decode(right_in[3, rows, :])
+            return carry
+
+        def right_side(n, carry):
+            rows = pl.ds(pl.multiple_of(n * RIGHT_CHUNK, RIGHT_CHUNK), RIGHT_CHUNK)
             right_arrival(2, n).wait_recv()
-            right_arrival(3, n).wait_recv()
-            right[rows, :] = decode(right_in[2, rows, :]) + decode(right_in[3, rows, :])
+            right[rows, :] += decode(right_in[2, rows, :])
             return carry
 
         def left_add(n, carry):
-            rows = pl.ds(pl.multiple_of(n * LEFT_CHUNK, LEFT_CHUNK), LEFT_CHUNK)
+            rows = left_rows(n)
             total = jnp.where(counts(row), left[rows, :], 0.0)
-            for slot in range(7):
+            for slot in range(4):
+                there = lax.rem(row - core + 2 * slot, ROWS)
+                some = counts(sibling) if slot == 0 else counts(there) | counts(there + 1)
                 left_arrival(slot, n).wait_recv()
-                total = total + jnp.where(
-                    counts(lax.rem(row + slot + 1, ROWS)), decode(left_in[slot, rows, :]), 0.0
-                )
+                total = total + jnp.where(some, decode(left_in[slot, rows, :]), 0.0)
             left[rows, :] = total
             return carry
 
         lax.fori_loop(0, RIGHT_CHUNKS, right_near, 0)
+
+        @pl.when(core == 0)
+        def _():
+            lax.fori_loop(0, RIGHT_CHUNKS, right_side, 0)
+
         lax.fori_loop(0, LEFT_CHUNKS, left_add, 0)
 
         for b, rows in enumerate(blocks):
@@ -322,18 +433,43 @@
 
     @pl.when(jnp.logical_not(is_owner))
     def _():
-        for n in range(LEFT_CHUNKS):
+        def given(n, carry):
+            share_copy(n).wait_send()
+            return carry
+
+        first = jnp.where(at_owner_chip, 0, (1 - core) * HALF_CHUNKS)
+        last = jnp.where(at_owner_chip, LEFT_CHUNKS, (2 - core) * HALF_CHUNKS)
+        lax.fori_loop(first, last, given, 0)
+
+    @pl.when(jnp.logical_not(at_owner_chip))
+    def _():
+        def handed_over(n, carry):
             left_copy(n).wait_send()
+            return carry
+
+        lax.fori_loop(core * HALF_CHUNKS, (core + 1) * HALF_CHUNKS, handed_over, 0)
+
+
+def put_out(diag, prob, outside_out, prob_out, sem):
+    copies = [
+        pltpu.make_async_copy(src, dst, sem.at[n])
+        for n, (src, dst) in enumerate(((diag, outside_out), (prob, prob_out)))
+    ]
+    for copy in copies:
+        copy.start()
+    for copy in copies:
+        copy.wait()
 
 
 def per_device(*args):
     vmem = pl.BlockSpec(memory_space=pltpu.VMEM)
-    anywhere = pl.BlockSpec(memory_space=pl.ANY)
-    tile = jax.ShapeDtypeStruct((BLK, BLK), jnp.float32)
-    return pl.pallas_call(
+    smem = pl.BlockSpec(memory_space=pltpu.SMEM)
+    hbm = pl.BlockSpec(memory_space=pltpu.HBM)
+    tile = pltpu.VMEM((BLK, BLK), jnp.float32)
+    results = pl.pallas_call(
         kernel,
         out_shape=(tile, tile),
-        in_specs=[anywhere] * 11,
+        in_specs=[hbm] * 9 + [smem] * 2,
         out_specs=(vmem, vmem),
         scratch_shapes=[
             pltpu.VMEM((BLK, BLK), jnp.bfloat16),
@@ -345,25 +481,35 @@
             pltpu.SMEM((4, 4), jnp.int32),
             pltpu.SMEM((4,), jnp.float32),
             pltpu.SMEM((4, 4), jnp.float32),
-            pltpu.SMEM((1,), jnp.int32),
-            pltpu.SMEM((1,), jnp.float32),
             pltpu.VMEM((BLK, BLK), jnp.float32),
             pltpu.VMEM((BLK, BLK), jnp.float32),
             pltpu.VMEM((BLK, BLK), jnp.int16),
             pltpu.VMEM((BLK, BLK), jnp.int16),
             pltpu.VMEM((4, BLK, BLK), jnp.int16),
-            pltpu.VMEM((7, BLK, BLK), jnp.int16),
+            pltpu.VMEM((4, BLK, BLK), jnp.int16),
             pltpu.SemaphoreType.DMA((11,)),
             pltpu.SemaphoreType.DMA((RIGHT_CHUNKS,)),
             pltpu.SemaphoreType.DMA((4, RIGHT_CHUNKS)),
             pltpu.SemaphoreType.DMA((LEFT_CHUNKS,)),
-            pltpu.SemaphoreType.DMA((7, LEFT_CHUNKS)),
+            pltpu.SemaphoreType.DMA((LEFT_CHUNKS,)),
+            pltpu.SemaphoreType.DMA((4, LEFT_CHUNKS)),
+            pltpu.SemaphoreType.REGULAR,
         ],
         compiler_params=pltpu.CompilerParams(
-            collective_id=0, has_side_effects=True, vmem_limit_bytes=62 * 1024 * 1024
+            collective_id=0, has_side_effects=True, vmem_limit_bytes=62400 * 1024
         ),
         name="outside_window",
     )(*args)
+    tile = jax.ShapeDtypeStruct((BLK, BLK), jnp.float32)
+    return pl.pallas_call(
+        put_out,
+        out_shape=(tile, tile),
+        in_specs=[vmem] * 2,
+        out_specs=(hbm, hbm),
+        scratch_shapes=[pltpu.SemaphoreType.DMA((2,))],
+        compiler_params=pltpu.CompilerParams(vmem_limit_bytes=1024 * 1024),
+        name="put_out",
+    )(*results)
 
 
 def solution(mesh):

time: 42.4 us -> 30.6 us (0.72)
  Pallas kernels: 36.8 us -> 28.6 us
  local copies, waits for them, and re-layouts: 3.32 us -> 0 us
    pallas_call x1 -> x2, Pallas kernels: 36.8 us -> 28.6 us  [the longest x1 27.2 us: per_device(): pl.pallas_call(kernel, out_shape=(tile, tile), in_specs=[hbm] * 9 + [smem...]
    unnamed x4 -> x0, local copies, waits for them, and re-layouts: 3.32 us -> none
where the time goes in v2:
time: 30.6 us; the launch traced here: 30.5 us
  Pallas kernels  28.6 us (93%)
  between operations  1.93 us (6%)
    pallas_call x1, Pallas kernels, per_device(): pl.pallas_call(kernel, out_shape=(tile, tile), in_specs=[hbm] * 9 + [smem...  27.2 us
    pallas_call x1, Pallas kernels, per_device(): pl.pallas_call(put_out, out_shape=(tile, tile), in_specs=[vmem] * 2, out_...  1.33 us

profile of v2, /device:TPU:6, one launch (start us, length us, event | category | flops | bytes accessed | tf_op | source)
XLA Modules:
  0.0 30.5 jit_solution(5067947779923467764)
XLA Ops:
  1.9 27.2 %outside_window.1 = (f32[512,512]{1,0:T(8,128)S(1)}, f32[512,512]{1,0:T(8,128)S(1)}) custom-call(bf16[512,512]{1,0:T(8,128)(2,1)} %outside.1, bf16[512,512]{1,0:T(8,128)(2,1)} %inside_head.1, bf16[512,512]{1,0:T(8,128)(2,1)} %inside_tail.1, f32[512,512]{1,0:T(8,128)} %inside_pair.1, s32[1,512]{1,0:T(1,128)} %seq_head_any.1, s32[1,512]{1,0:T(1,128)} %seq_tail_any.1, ...), custom_call_target="tpu_custom_call" | custom-call | tf_op jit(solution)/shard_map/outside_window/pallas_call | solution.py:469
  29.1 1.3 %put_out.1 = (f32[512,512]{1,0:T(8,128)}, f32[512,512]{1,0:T(8,128)}) custom-call(f32[512,512]{1,0:T(8,128)S(1)} %get-tuple-element.4.diag, f32[512,512]{1,0:T(8,128)S(1)} %get-tuple-element.5.prob), custom_call_target="tpu_custom_call" | custom-call | tf_op jit(solution)/shard_map/put_out/pallas_call | solution.py:504

commit v3 on v2

--- a/solution.py
+++ b/solution.py
@@ -14,14 +14,13 @@
 COLS = 32
 RIGHT_CHUNK = 32
 RIGHT_CHUNKS = BLK // RIGHT_CHUNK
-AHEAD = 2
-FIRST_ROWS = 128
+SHORT = 5
 LEFT_CHUNK = 64
 LEFT_CHUNKS = BLK // LEFT_CHUNK
 HALF_CHUNKS = LEFT_CHUNKS // 2
 
 LOG_LOW = math.log(BLK * 0.0099**2) - 0.01
-LOG_HIGH = math.log(3 * BLK * 17.5**2) + 0.01
+LOG_HIGH = math.log(5 * BLK * 17.5**2) + 0.01
 LOG_MIDDLE = (LOG_LOW + LOG_HIGH) / 2
 LOG_STEP = (LOG_HIGH - LOG_LOW) / 65534
 
@@ -53,6 +52,8 @@
     head_tile,
     tail_tile,
     factor,
+    right_weight,
+    left_weight,
     seq_head,
     seq_tail,
     pair_mask,
@@ -82,6 +83,7 @@
     chip_away = lax.rem(row // 2 - owner_row // 2 + 4, 4)
     at_owner_chip = chip_away == 0
     sibling = row + 1 - 2 * core
+    early = owner_row < 4
 
     def at_col(c):
         return (row, lax.rem(c + COLS, COLS))
@@ -89,21 +91,15 @@
     def at_row(r):
         return (lax.rem(r + ROWS, ROWS), col)
 
-    gathers = is_owner & (core == 1)
-    near = (along == 0) & (core == 1)
-    has_up = (along == 2) | (along == 3) | (along == 6) | (along == 7) | gathers
-    passes_on = (along >= 3) & (along <= 6)
-    next_col = jnp.where(
-        passes_on | near, jnp.where((along == 3) | (along == 4), col - 1, col + 1), col - reach
-    )
-    next_slot = jnp.where(
-        passes_on | (along == 2), 0, jnp.where(along == 7, 1, jnp.where(is_owner, 3, 2))
-    )
-    up_slot = jnp.where(gathers, 2, 0)
-    far = (along == 4) | (along == 5)
-    middle = (along == 3) | (along == 6)
-    last = (along == 2) | (along == 7)
-    far_col = jnp.where(along == 4, col - 2, col + 2)
+    upward = (along >= 5) | (along == 0)
+    depth = jnp.where(upward, 9 - along, along)
+    toward = jnp.where(upward, col + 1, col - 1)
+    behind = jnp.where(upward, col - 1, col + 1)
+    first_tile, second_tile, third_tile = depth == 2, depth == 3, depth == 4
+    beside = along <= 1
+    beside_col = jnp.where(along == 0, col - 1, jnp.where(core == 0, col + 1, col - 7))
+    next_col = jnp.where(beside, beside_col, jnp.where(first_tile, col - reach, toward))
+    next_slot = jnp.where(beside | (first_tile & upward), 1, 0)
 
     loads = [
         pltpu.make_async_copy(src, dst, load_sem.at[n])
@@ -119,115 +115,113 @@
     def announce(device):
         pl.semaphore_signal(barrier, inc=1, device_id=device, device_id_type=MESH)
 
-    @pl.when(has_up)
-    def _():
-        announce(at_col(jnp.where((along == 2) | (along == 3), col + 1, col - 1)))
-
-    @pl.when(last)
-    def _():
-        announce(at_col(jnp.where(along == 2, col + 2, col - 2)))
+    @pl.when(first_tile | second_tile | third_tile)
+    def _():
+        announce(at_col(behind))
+
+    @pl.when(first_tile)
+    def _():
+        announce(at_col(jnp.where(along == 7, col + 1, jnp.where(core == 0, col - 1, col + 7))))
 
     @pl.when(is_owner)
     def _():
-        for away in (2 - core, 7 - core, 8):
+        for away in (2 - core, 7 - core):
             announce(at_col(col + away))
 
-    @pl.when(is_owner & (core == 0))
-    def _():
-        announce(at_col(col + 1))
-
     @pl.when(jnp.logical_not(at_owner_chip & jnp.logical_not(is_owner)))
     def _():
         announce(at_row(sibling))
 
-    @pl.when(jnp.logical_not(at_owner_chip))
+    @pl.when(jnp.logical_not(at_owner_chip | early))
     def _():
         announce(at_row(owner_row))
+
+    @pl.when(is_owner & early)
+    def _():
+        for away in range(2, ROWS):
+            announce(at_row(row - core + away))
 
     loads[0].wait()
     loads[1].wait()
 
-    def right_product(rows):
-        right[rows, :] = lax.dot_general(
-            out_tile[rows, :],
-            tail_tile[...],
-            (((1,), (1,)), ((), ())),
-            preferred_element_type=jnp.float32,
-        )
-
-    right_product(slice(0, FIRST_ROWS))
-
-    pl.semaphore_wait(barrier, jnp.where(is_owner, ROWS - 1, jnp.where(far, 3, 2)))
-
-    @pl.when(is_owner)
+    right[...] = lax.dot_general(
+        out_tile[...],
+        tail_tile[...],
+        (((1,), (1,)), ((), ())),
+        preferred_element_type=jnp.float32,
+    )
+
+    others = jnp.where(third_tile, 3, 2) + jnp.where(early & jnp.logical_not(at_owner_chip), 1, 0)
+    pl.semaphore_wait(barrier, jnp.where(is_owner, jnp.where(early, 1, ROWS - 1), others))
+
+    @pl.when(is_owner & jnp.logical_not(early))
     def _():
         for away in range(2, ROWS):
             pl.semaphore_signal(
                 left_ready, inc=1, device_id=at_row(row - core + away), device_id_type=MESH
             )
 
+    def right_rows(n):
+        return pl.ds(pl.multiple_of(n * RIGHT_CHUNK, RIGHT_CHUNK), RIGHT_CHUNK)
+
     def right_copy(n):
-        rows = pl.ds(pl.multiple_of(n * RIGHT_CHUNK, RIGHT_CHUNK), RIGHT_CHUNK)
         return pltpu.make_async_remote_copy(
-            src_ref=right_code.at[rows],
-            dst_ref=right_in.at[next_slot, rows],
+            src_ref=right_code.at[right_rows(n)],
+            dst_ref=right_in.at[next_slot, right_rows(n)],
             send_sem=right_send.at[n],
             recv_sem=right_recv.at[next_slot, n],
             device_id=at_col(next_col),
             device_id_type=MESH,
         )
 
-    def ahead_copy(n):
-        rows = pl.ds(pl.multiple_of(n * RIGHT_CHUNK, RIGHT_CHUNK), RIGHT_CHUNK)
+    def across_copy(n):
         return pltpu.make_async_remote_copy(
-            src_ref=right_code.at[rows],
-            dst_ref=right_in.at[1, rows],
+            src_ref=right_code.at[right_rows(n)],
+            dst_ref=right_in.at[0, right_rows(n)],
             send_sem=right_send.at[n],
-            recv_sem=right_recv.at[1, n],
-            device_id=at_col(far_col),
+            recv_sem=right_recv.at[0, n],
+            device_id=at_col(behind),
             device_id_type=MESH,
         )
 
     def right_arrival(slot, n):
-        rows = pl.ds(pl.multiple_of(n * RIGHT_CHUNK, RIGHT_CHUNK), RIGHT_CHUNK)
         return pltpu.make_async_remote_copy(
-            src_ref=right_code.at[rows],
-            dst_ref=right_in.at[slot, rows],
+            src_ref=right_code.at[right_rows(n)],
+            dst_ref=right_in.at[slot, right_rows(n)],
             send_sem=right_send.at[n],
             recv_sem=right_recv.at[slot, n],
             device_id=at_col(next_col),
             device_id_type=MESH,
         )
 
-    def code_rows(n):
-        rows = pl.ds(pl.multiple_of(n * RIGHT_CHUNK, RIGHT_CHUNK), RIGHT_CHUNK)
-        right_code[rows, :] = encode(right[rows, :])
-
-    def send_own(n, carry):
-        code_rows(n)
+    def chunk(m):
+        return jnp.where(upward, RIGHT_CHUNKS - 1 - m, m)
+
+    def send_across(m, carry):
+        n = chunk(SHORT - 1 - m)
+        right_code[right_rows(n), :] = encode(right[right_rows(n), :])
+        across_copy(n).start()
+        return carry
+
+    def send_own(m, carry):
+        n = chunk(m)
+        right_code[right_rows(n), :] = encode(right[right_rows(n), :])
         right_copy(n).start()
         return carry
 
-    def send_ahead(n, carry):
-        code_rows(n)
-        ahead_copy(n).start()
-        return carry
-
-    first_chunks = FIRST_ROWS // RIGHT_CHUNK
-
-    @pl.when(far)
-    def _():
-        lax.fori_loop(0, AHEAD, send_ahead, 0)
-
-    starts = jnp.logical_not(has_up)
-    lax.fori_loop(
-        jnp.where(far, AHEAD, 0),
-        jnp.where(starts, first_chunks, jnp.where(middle, AHEAD, 0)),
-        send_own,
+    @pl.when(third_tile)
+    def _():
+        lax.fori_loop(0, SHORT, send_across, 0)
+
+    own_from = jnp.where(third_tile, SHORT, 0)
+    own_to = jnp.where(
+        first_tile,
         0,
+        jnp.where(
+            second_tile, SHORT, jnp.where(third_tile, RIGHT_CHUNKS - SHORT, RIGHT_CHUNKS)
+        ),
     )
-    right_product(slice(FIRST_ROWS, BLK))
-    lax.fori_loop(first_chunks, jnp.where(starts, RIGHT_CHUNKS, first_chunks), send_own, 0)
+    lax.fori_loop(own_from, own_to, send_own, 0)
 
     loads[2].wait()
 
@@ -278,7 +272,11 @@
     @pl.when(jnp.logical_not(at_owner_chip))
     def _():
         mine, theirs = counts(row), counts(sibling)
-        pl.semaphore_wait(left_ready, 1)
+
+        @pl.when(jnp.logical_not(early))
+        def _():
+            pl.semaphore_wait(left_ready, 1)
+
 
         def merge(n, carry):
             rows = left_rows(n)
@@ -291,29 +289,31 @@
 
         lax.fori_loop(core * HALF_CHUNKS, (core + 1) * HALF_CHUNKS, merge, 0)
 
-    @pl.when(last)
-    def _():
-        def step(n, carry):
-            rows = pl.ds(pl.multiple_of(n * RIGHT_CHUNK, RIGHT_CHUNK), RIGHT_CHUNK)
-            right_arrival(0, n).wait_recv()
-            right_arrival(1, n).wait_recv()
-            total = right[rows, :] + decode(right_in[0, rows, :]) + decode(right_in[1, rows, :])
-            right_code[rows, :] = encode(total)
-            right_copy(n).start()
-            return carry
-
-        lax.fori_loop(0, AHEAD, step, 0)
-
-    @pl.when(has_up)
-    def _():
-        def step(n, carry):
-            rows = pl.ds(pl.multiple_of(n * RIGHT_CHUNK, RIGHT_CHUNK), RIGHT_CHUNK)
-            right_arrival(up_slot, n).wait_recv()
-            right_code[rows, :] = encode(right[rows, :] + decode(right_in[up_slot, rows, :]))
-            right_copy(n).start()
-            return carry
-
-        lax.fori_loop(jnp.where(gathers, 0, AHEAD), RIGHT_CHUNKS, step, 0)
+    def pass_on(m, carry):
+        n = chunk(m)
+        rows = right_rows(n)
+        right_arrival(0, n).wait_recv()
+        right_code[rows, :] = encode(right[rows, :] + decode(right_in[0, rows, :]))
+        right_copy(n).start()
+        return carry
+
+    def pass_on_both(m, carry):
+        n = chunk(m)
+        rows = right_rows(n)
+        right_arrival(1, n).wait_recv()
+        total = right[rows, :] + decode(right_in[1, rows, :])
+        right_arrival(0, n).wait_recv()
+        right_code[rows, :] = encode(total + decode(right_in[0, rows, :]))
+        right_copy(n).start()
+        return carry
+
+    @pl.when(first_tile)
+    def _():
+        lax.fori_loop(0, RIGHT_CHUNKS, pass_on_both, 0)
+
+    @pl.when(second_tile | third_tile)
+    def _():
+        lax.fori_loop(own_to, RIGHT_CHUNKS, pass_on, 0)
 
     @pl.when(jnp.logical_not(is_owner))
     def _():
@@ -355,8 +355,8 @@
         lane = lax.broadcasted_iota(jnp.int32, (1, BLK), 1)
         span_nt = BLK * span_blocks[0].astype(jnp.float32)
 
-        blocks = [slice(n * 128, n * 128 + 128) for n in range(4)]
-        for rows in blocks:
+        for b in range(4):
+            rows = slice(b * 128, b * 128 + 128)
             codes = head_codes[rows]
             table = chosen(codes, pair_rows)
             place = lax.broadcasted_iota(jnp.int32, (128, BLK), 0) + rows.start
@@ -364,6 +364,10 @@
             span = span_nt + (across - place).astype(jnp.float32)
             penalty = jnp.sqrt(64.0 * BLK / span)
             factor[rows, :] = factor[rows, :] * table * penalty / partition[0]
+            allowed = chosen(lane // 128, [pair_mask[b, n].astype(jnp.float32) for n in range(4)])
+            allowed = allowed * (1.0 / BLK)
+            right_weight[rows, :] = jnp.broadcast_to(allowed * tail_weight, (128, BLK))
+            left_weight[rows, :] = allowed * chosen(codes, weights)
 
         def left_arrival(slot, n):
             return pltpu.make_async_remote_copy(
@@ -375,16 +379,22 @@
                 device_id_type=MESH,
             )
 
-        def right_near(n, carry):
-            rows = pl.ds(pl.multiple_of(n * RIGHT_CHUNK, RIGHT_CHUNK), RIGHT_CHUNK)
-            right_arrival(3, n).wait_recv()
-            right[rows, :] = decode(right_in[3, rows, :])
-            return carry
-
-        def right_side(n, carry):
-            rows = pl.ds(pl.multiple_of(n * RIGHT_CHUNK, RIGHT_CHUNK), RIGHT_CHUNK)
-            right_arrival(2, n).wait_recv()
-            right[rows, :] += decode(right_in[2, rows, :])
+        def arrive(slot, n):
+            right_arrival(slot, n).wait_recv()
+            return decode(right_in[slot, right_rows(n), :])
+
+        def half_way(m, carry):
+            for slot, n in ((0, m), (1, RIGHT_CHUNKS - 1 - m)):
+                right[right_rows(n), :] = arrive(slot, n)
+            return carry
+
+        def finish(m, carry):
+            for slot, n in ((0, m), (1, RIGHT_CHUNKS - 1 - m)):
+                rows = right_rows(n)
+                right_sum = right[rows, :] + arrive(slot, n)
+                diag = right_sum * right_weight[rows, :] + left[rows, :]
+                outside_out[rows, :] = diag
+                prob_out[rows, :] = diag * factor[rows, :]
             return carry
 
         def left_add(n, carry):
@@ -395,35 +405,13 @@
                 some = counts(sibling) if slot == 0 else counts(there) | counts(there + 1)
                 left_arrival(slot, n).wait_recv()
                 total = total + jnp.where(some, decode(left_in[slot, rows, :]), 0.0)
-            left[rows, :] = total
-            return carry
-
-        lax.fori_loop(0, RIGHT_CHUNKS, right_near, 0)
-
-        @pl.when(core == 0)
-        def _():
-            lax.fori_loop(0, RIGHT_CHUNKS, right_side, 0)
+            left[rows, :] = total * left_weight[rows, :]
+            return carry
 
         lax.fori_loop(0, LEFT_CHUNKS, left_add, 0)
 
-        for b, rows in enumerate(blocks):
-            codes = head_codes[rows]
-            head_weight = chosen(codes, weights)
-            allowed = chosen(lane // 128, [pair_mask[b, n].astype(jnp.float32) for n in range(4)])
-            for part in range(128 // RIGHT_CHUNK):
-                n = b * (128 // RIGHT_CHUNK) + part
-                here = slice(n * RIGHT_CHUNK, (n + 1) * RIGHT_CHUNK)
-                inner = slice(part * RIGHT_CHUNK, (part + 1) * RIGHT_CHUNK)
-                right_arrival(0, n).wait_recv()
-                right_arrival(1, n).wait_recv()
-                right_sum = right[here, :] + decode(right_in[0, here, :]) + decode(right_in[1, here, :])
-                diag = (
-                    allowed
-                    * (right_sum * tail_weight + head_weight[inner] * left[here, :])
-                    * (1.0 / BLK)
-                )
-                outside_out[here, :] = diag
-                prob_out[here, :] = diag * factor[here, :]
+        lax.fori_loop(0, RIGHT_CHUNKS // 2, half_way, 0)
+        lax.fori_loop(RIGHT_CHUNKS // 2, RIGHT_CHUNKS, finish, 0)
 
     def sent(n, carry):
         right_copy(n).wait_send()
@@ -476,6 +464,8 @@
             pltpu.VMEM((BLK, BLK), jnp.bfloat16),
             pltpu.VMEM((BLK, BLK), jnp.bfloat16),
             pltpu.VMEM((BLK, BLK), jnp.float32),
+            pltpu.VMEM((BLK, BLK), jnp.float32),
+            pltpu.VMEM((BLK, BLK), jnp.float32),
             pltpu.VMEM((1, BLK), jnp.int32),
             pltpu.VMEM((1, BLK), jnp.int32),
             pltpu.SMEM((4, 4), jnp.int32),
@@ -485,11 +475,11 @@
             pltpu.VMEM((BLK, BLK), jnp.float32),
             pltpu.VMEM((BLK, BLK), jnp.int16),
             pltpu.VMEM((BLK, BLK), jnp.int16),
-            pltpu.VMEM((4, BLK, BLK), jnp.int16),
+            pltpu.VMEM((2, BLK, BLK), jnp.int16),
             pltpu.VMEM((4, BLK, BLK), jnp.int16),
             pltpu.SemaphoreType.DMA((11,)),
             pltpu.SemaphoreType.DMA((RIGHT_CHUNKS,)),
-            pltpu.SemaphoreType.DMA((4, RIGHT_CHUNKS)),
+            pltpu.SemaphoreType.DMA((2, RIGHT_CHUNKS)),
             pltpu.SemaphoreType.DMA((LEFT_CHUNKS,)),
             pltpu.SemaphoreType.DMA((LEFT_CHUNKS,)),
             pltpu.SemaphoreType.DMA((4, LEFT_CHUNKS)),

time: 30.6 us -> 29.6 us (0.967)
  Pallas kernels: 28.6 us -> 27.5 us
    pallas_call x1, Pallas kernels: 27.2 us -> 26.1 us  [per_device(): pl.pallas_call(kernel, out_shape=(tile, tile), in_specs=[hbm] * 9 + [smem...]
where the time goes in v3:
time: 29.6 us; the launch traced here: 29.4 us
  Pallas kernels  27.5 us (93%)
  between operations  1.93 us (7%)
    pallas_call x1, Pallas kernels, per_device(): pl.pallas_call(kernel, out_shape=(tile, tile), in_specs=[hbm] * 9 + [smem...  26.1 us
    pallas_call x1, Pallas kernels, per_device(): pl.pallas_call(put_out, out_shape=(tile, tile), in_specs=[vmem] * 2, out_...  1.33 us

profile of v3, /device:TPU:6, one launch (start us, length us, event | category | flops | bytes accessed | tf_op | source)
XLA Modules:
  0.0 29.4 jit_solution(3831399875207187575)
XLA Ops:
  1.9 26.1 %outside_window.1 = (f32[512,512]{1,0:T(8,128)S(1)}, f32[512,512]{1,0:T(8,128)S(1)}) custom-call(bf16[512,512]{1,0:T(8,128)(2,1)} %outside.1, bf16[512,512]{1,0:T(8,128)(2,1)} %inside_head.1, bf16[512,512]{1,0:T(8,128)(2,1)} %inside_tail.1, f32[512,512]{1,0:T(8,128)} %inside_pair.1, s32[1,512]{1,0:T(1,128)} %seq_head_any.1, s32[1,512]{1,0:T(1,128)} %seq_tail_any.1, ...), custom_call_target="tpu_custom_call" | custom-call | tf_op jit(solution)/shard_map/outside_window/pallas_call | solution.py:457
  28.1 1.3 %put_out.1 = (f32[512,512]{1,0:T(8,128)}, f32[512,512]{1,0:T(8,128)}) custom-call(f32[512,512]{1,0:T(8,128)S(1)} %get-tuple-element.4.diag, f32[512,512]{1,0:T(8,128)S(1)} %get-tuple-element.5.prob), custom_call_target="tpu_custom_call" | custom-call | tf_op jit(solution)/shard_map/put_out/pallas_call | solution.py:494

commit v4 on v3

--- a/solution.py
+++ b/solution.py
@@ -72,6 +72,7 @@
     left_send,
     left_recv,
     left_ready,
+    chain_ready,
 ):
     row = lax.axis_index("row")
     col = lax.axis_index("col")
@@ -84,6 +85,10 @@
     at_owner_chip = chip_away == 0
     sibling = row + 1 - 2 * core
     early = owner_row < 4
+    chip_row = row // 2
+    waits = (owner_row == 0) & (chip_row >= 2)
+    tells = ((chip_row == 2) & (along == 3)) | ((chip_row == 3) & is_owner)
+    told_col = jnp.where(is_owner, col + 2 - core, col + 1)
 
     def at_col(c):
         return (row, lax.rem(c + COLS, COLS))
@@ -98,8 +103,12 @@
     first_tile, second_tile, third_tile = depth == 2, depth == 3, depth == 4
     beside = along <= 1
     beside_col = jnp.where(along == 0, col - 1, jnp.where(core == 0, col + 1, col - 7))
+    wraps = row < 2
+    straight = wraps & (along == 0)
+    joined = first_tile & jnp.logical_not(wraps & (along == 7))
+    beside_col = jnp.where(straight, col - reach, beside_col)
     next_col = jnp.where(beside, beside_col, jnp.where(first_tile, col - reach, toward))
-    next_slot = jnp.where(beside | (first_tile & upward), 1, 0)
+    next_slot = jnp.where(straight, 2, jnp.where(beside | (first_tile & upward), 1, 0))
 
     loads = [
         pltpu.make_async_copy(src, dst, load_sem.at[n])
@@ -115,18 +124,29 @@
     def announce(device):
         pl.semaphore_signal(barrier, inc=1, device_id=device, device_id_type=MESH)
 
-    @pl.when(first_tile | second_tile | third_tile)
+    @pl.when((first_tile | second_tile | third_tile) & jnp.logical_not(tells))
     def _():
         announce(at_col(behind))
 
-    @pl.when(first_tile)
+    @pl.when(waits)
+    def _():
+        announce(at_col(next_col))
+
+    @pl.when(is_owner & wraps)
+    def _():
+        announce(at_col(col + 8 - core))
+
+    @pl.when(joined)
     def _():
         announce(at_col(jnp.where(along == 7, col + 1, jnp.where(core == 0, col - 1, col + 7))))
 
     @pl.when(is_owner)
     def _():
-        for away in (2 - core, 7 - core):
-            announce(at_col(col + away))
+        announce(at_col(col + 7 - core))
+
+    @pl.when(is_owner & jnp.logical_not(tells))
+    def _():
+        announce(at_col(col + 2 - core))
 
     @pl.when(jnp.logical_not(at_owner_chip & jnp.logical_not(is_owner)))
     def _():
@@ -152,7 +172,12 @@
     )
 
     others = jnp.where(third_tile, 3, 2) + jnp.where(early & jnp.logical_not(at_owner_chip), 1, 0)
-    pl.semaphore_wait(barrier, jnp.where(is_owner, jnp.where(early, 1, ROWS - 1), others))
+    arrivals = jnp.where(is_owner, jnp.where(early, 1, ROWS - 1), others)
+    pl.semaphore_wait(barrier, arrivals + jnp.where(tells, 1, 0) - jnp.where(waits, 1, 0))
+
+    @pl.when(tells)
+    def _():
+        pl.semaphore_signal(chain_ready, inc=1, device_id=at_col(told_col), device_id_type=MESH)
 
     @pl.when(is_owner & jnp.logical_not(early))
     def _():
@@ -208,6 +233,78 @@
         right_code[right_rows(n), :] = encode(right[right_rows(n), :])
         right_copy(n).start()
         return carry
+
+    def counts(r):
+        return col >= lax.rem(col - r + 31, 8) + 1
+
+    def left_rows(n):
+        return pl.ds(pl.multiple_of(n * LEFT_CHUNK, LEFT_CHUNK), LEFT_CHUNK)
+
+    def share_copy(n):
+        return pltpu.make_async_remote_copy(
+            src_ref=left_code.at[left_rows(n)],
+            dst_ref=left_in.at[0, left_rows(n)],
+            send_sem=share_send.at[n],
+            recv_sem=left_recv.at[0, n],
+            device_id=at_row(sibling),
+            device_id_type=MESH,
+        )
+
+    def left_copy(n):
+        return pltpu.make_async_remote_copy(
+            src_ref=left_code.at[left_rows(n)],
+            dst_ref=left_in.at[chip_away, left_rows(n)],
+            send_sem=left_send.at[n],
+            recv_sem=left_recv.at[chip_away, n],
+            device_id=at_row(owner_row),
+            device_id_type=MESH,
+        )
+
+    def left_part():
+        loads[2].wait()
+
+        left[...] = lax.dot_general(
+            head_tile[...],
+            out_tile[...],
+            (((0,), (0,)), ((), ())),
+            preferred_element_type=jnp.float32,
+        )
+
+        @pl.when(jnp.logical_not(is_owner))
+        def _():
+            def give(n, carry):
+                left_code[left_rows(n), :] = encode(left[left_rows(n), :])
+                share_copy(n).start()
+                return carry
+
+            first = jnp.where(at_owner_chip, 0, (1 - core) * HALF_CHUNKS)
+            last = jnp.where(at_owner_chip, LEFT_CHUNKS, (2 - core) * HALF_CHUNKS)
+            lax.fori_loop(first, last, give, 0)
+
+        @pl.when(jnp.logical_not(at_owner_chip))
+        def _():
+            mine, theirs = counts(row), counts(sibling)
+
+            @pl.when(jnp.logical_not(early))
+            def _():
+                pl.semaphore_wait(left_ready, 1)
+
+
+            def merge(n, carry):
+                rows = left_rows(n)
+                share_copy(n).wait_recv()
+                total = jnp.where(mine, left[rows, :], 0.0)
+                total = total + jnp.where(theirs, decode(left_in[0, rows, :]), 0.0)
+                left_code[rows, :] = encode(jnp.where(mine | theirs, total, 1.0))
+                left_copy(n).start()
+                return carry
+
+            lax.fori_loop(core * HALF_CHUNKS, (core + 1) * HALF_CHUNKS, merge, 0)
+
+    @pl.when(waits)
+    def _():
+        left_part()
+        pl.semaphore_wait(chain_ready, 1)
 
     @pl.when(third_tile)
     def _():
@@ -223,71 +320,9 @@
     )
     lax.fori_loop(own_from, own_to, send_own, 0)
 
-    loads[2].wait()
-
-    left[...] = lax.dot_general(
-        head_tile[...],
-        out_tile[...],
-        (((0,), (0,)), ((), ())),
-        preferred_element_type=jnp.float32,
-    )
-
-    def counts(r):
-        return col >= lax.rem(col - r + 31, 8) + 1
-
-    def left_rows(n):
-        return pl.ds(pl.multiple_of(n * LEFT_CHUNK, LEFT_CHUNK), LEFT_CHUNK)
-
-    def share_copy(n):
-        return pltpu.make_async_remote_copy(
-            src_ref=left_code.at[left_rows(n)],
-            dst_ref=left_in.at[0, left_rows(n)],
-            send_sem=share_send.at[n],
-            recv_sem=left_recv.at[0, n],
-            device_id=at_row(sibling),
-            device_id_type=MESH,
-        )
-
-    def left_copy(n):
-        return pltpu.make_async_remote_copy(
-            src_ref=left_code.at[left_rows(n)],
-            dst_ref=left_in.at[chip_away, left_rows(n)],
-            send_sem=left_send.at[n],
-            recv_sem=left_recv.at[chip_away, n],
-            device_id=at_row(owner_row),
-            device_id_type=MESH,
-        )
-
-    @pl.when(jnp.logical_not(is_owner))
-    def _():
-        def give(n, carry):
-            left_code[left_rows(n), :] = encode(left[left_rows(n), :])
-            share_copy(n).start()
-            return carry
-
-        first = jnp.where(at_owner_chip, 0, (1 - core) * HALF_CHUNKS)
-        last = jnp.where(at_owner_chip, LEFT_CHUNKS, (2 - core) * HALF_CHUNKS)
-        lax.fori_loop(first, last, give, 0)
-
-    @pl.when(jnp.logical_not(at_owner_chip))
-    def _():
-        mine, theirs = counts(row), counts(sibling)
-
-        @pl.when(jnp.logical_not(early))
-        def _():
-            pl.semaphore_wait(left_ready, 1)
-
-
-        def merge(n, carry):
-            rows = left_rows(n)
-            share_copy(n).wait_recv()
-            total = jnp.where(mine, left[rows, :], 0.0)
-            total = total + jnp.where(theirs, decode(left_in[0, rows, :]), 0.0)
-            left_code[rows, :] = encode(jnp.where(mine | theirs, total, 1.0))
-            left_copy(n).start()
-            return carry
-
-        lax.fori_loop(core * HALF_CHUNKS, (core + 1) * HALF_CHUNKS, merge, 0)
+    @pl.when(jnp.logical_not(waits))
+    def _():
+        left_part()
 
     def pass_on(m, carry):
         n = chunk(m)
@@ -307,11 +342,11 @@
         right_copy(n).start()
         return carry
 
-    @pl.when(first_tile)
+    @pl.when(joined)
     def _():
         lax.fori_loop(0, RIGHT_CHUNKS, pass_on_both, 0)
 
-    @pl.when(second_tile | third_tile)
+    @pl.when(jnp.logical_not(joined | beside))
     def _():
         lax.fori_loop(own_to, RIGHT_CHUNKS, pass_on, 0)
 
@@ -408,9 +443,14 @@
             left[rows, :] = total * left_weight[rows, :]
             return carry
 
+
+        def add_straight(n, carry):
+            right[right_rows(n), :] += arrive(2, n)
+            return carry
+
+        lax.fori_loop(0, RIGHT_CHUNKS // 2, half_way, 0)
+        lax.fori_loop(0, jnp.where(wraps, RIGHT_CHUNKS, 0), add_straight, 0)
         lax.fori_loop(0, LEFT_CHUNKS, left_add, 0)
-
-        lax.fori_loop(0, RIGHT_CHUNKS // 2, half_way, 0)
         lax.fori_loop(RIGHT_CHUNKS // 2, RIGHT_CHUNKS, finish, 0)
 
     def sent(n, carry):
@@ -475,14 +515,15 @@
             pltpu.VMEM((BLK, BLK), jnp.float32),
             pltpu.VMEM((BLK, BLK), jnp.int16),
             pltpu.VMEM((BLK, BLK), jnp.int16),
-            pltpu.VMEM((2, BLK, BLK), jnp.int16),
+            pltpu.VMEM((3, BLK, BLK), jnp.int16),
             pltpu.VMEM((4, BLK, BLK), jnp.int16),
             pltpu.SemaphoreType.DMA((11,)),
             pltpu.SemaphoreType.DMA((RIGHT_CHUNKS,)),
-            pltpu.SemaphoreType.DMA((2, RIGHT_CHUNKS)),
+            pltpu.SemaphoreType.DMA((3, RIGHT_CHUNKS)),
             pltpu.SemaphoreType.DMA((LEFT_CHUNKS,)),
             pltpu.SemaphoreType.DMA((LEFT_CHUNKS,)),
             pltpu.SemaphoreType.DMA((4, LEFT_CHUNKS)),
+            pltpu.SemaphoreType.REGULAR,
             pltpu.SemaphoreType.REGULAR,
         ],
         compiler_params=pltpu.CompilerParams(

time: 29.6 us -> 28.1 us (0.949)
  the two profiles are of different devices: /device:TPU:6 before, /device:TPU:24 now
where the time goes in v4:
time: 28.1 us; the launch traced here: 28 us
  Pallas kernels  26 us (93%)
  between operations  1.93 us (7%)
    pallas_call x1, Pallas kernels, per_device(): pl.pallas_call(kernel, out_shape=(tile, tile), in_specs=[hbm] * 9 + [smem...  24.7 us
    pallas_call x1, Pallas kernels, per_device(): pl.pallas_call(put_out, out_shape=(tile, tile), in_specs=[vmem] * 2, out_...  1.33 us

profile of v4, /device:TPU:24, one launch (start us, length us, event | category | flops | bytes accessed | tf_op | source)
XLA Modules:
  0.0 28.0 jit_solution(1277208422171621244)
XLA Ops:
  1.9 24.7 %outside_window.1 = (f32[512,512]{1,0:T(8,128)S(1)}, f32[512,512]{1,0:T(8,128)S(1)}) custom-call(bf16[512,512]{1,0:T(8,128)(2,1)} %outside.1, bf16[512,512]{1,0:T(8,128)(2,1)} %inside_head.1, bf16[512,512]{1,0:T(8,128)(2,1)} %inside_tail.1, f32[512,512]{1,0:T(8,128)} %inside_pair.1, s32[1,512]{1,0:T(1,128)} %seq_head_any.1, s32[1,512]{1,0:T(1,128)} %seq_tail_any.1, ...), custom_call_target="tpu_custom_call" | custom-call | tf_op jit(solution)/shard_map/outside_window/pallas_call | solution.py:497
  26.6 1.3 %put_out.1 = (f32[512,512]{1,0:T(8,128)}, f32[512,512]{1,0:T(8,128)}) custom-call(f32[512,512]{1,0:T(8,128)S(1)} %get-tuple-element.4.diag, f32[512,512]{1,0:T(8,128)S(1)} %get-tuple-element.5.prob), custom_call_target="tpu_custom_call" | custom-call | tf_op jit(solution)/shard_map/put_out/pallas_call | solution.py:535

commit v5 on v4

--- a/solution.py
+++ b/solution.py
@@ -104,8 +104,10 @@
     beside = along <= 1
     beside_col = jnp.where(along == 0, col - 1, jnp.where(core == 0, col + 1, col - 7))
     wraps = row < 2
-    straight = wraps & (along == 0)
-    joined = first_tile & jnp.logical_not(wraps & (along == 7))
+    lower = (core == 0) & (row >= 2)
+    straight = (wraps & (along == 0)) | (lower & (along == 1))
+    joined = first_tile & jnp.logical_not((wraps & (along == 7)) | (lower & (along == 2)))
+    takes_straight = wraps | lower
     beside_col = jnp.where(straight, col - reach, beside_col)
     next_col = jnp.where(beside, beside_col, jnp.where(first_tile, col - reach, toward))
     next_slot = jnp.where(straight, 2, jnp.where(beside | (first_tile & upward), 1, 0))
@@ -132,9 +134,9 @@
     def _():
         announce(at_col(next_col))
 
-    @pl.when(is_owner & wraps)
-    def _():
-        announce(at_col(col + 8 - core))
+    @pl.when(is_owner & takes_straight)
+    def _():
+        announce(at_col(jnp.where(wraps, col + 8 - core, col + 1)))
 
     @pl.when(joined)
     def _():
@@ -449,7 +451,7 @@
             return carry
 
         lax.fori_loop(0, RIGHT_CHUNKS // 2, half_way, 0)
-        lax.fori_loop(0, jnp.where(wraps, RIGHT_CHUNKS, 0), add_straight, 0)
+        lax.fori_loop(0, jnp.where(takes_straight, RIGHT_CHUNKS, 0), add_straight, 0)
         lax.fori_loop(0, LEFT_CHUNKS, left_add, 0)
         lax.fori_loop(RIGHT_CHUNKS // 2, RIGHT_CHUNKS, finish, 0)
 

time: 28.1 us -> 27.4 us (0.975)
  the two profiles are of different devices: /device:TPU:24 before, /device:TPU:6 now
where the time goes in v5:
time: 27.4 us; the launch traced here: 27.3 us
  Pallas kernels  25.4 us (93%)
  between operations  1.93 us (7%)
    pallas_call x1, Pallas kernels, per_device(): pl.pallas_call(kernel, out_shape=(tile, tile), in_specs=[hbm] * 9 + [smem...  24 us
    pallas_call x1, Pallas kernels, per_device(): pl.pallas_call(put_out, out_shape=(tile, tile), in_specs=[vmem] * 2, out_...  1.33 us

profile of v5, /device:TPU:6, one launch (start us, length us, event | category | flops | bytes accessed | tf_op | source)
XLA Modules:
  0.0 27.3 jit_solution(9545925629269247389)
XLA Ops:
  1.9 24.0 %outside_window.1 = (f32[512,512]{1,0:T(8,128)S(1)}, f32[512,512]{1,0:T(8,128)S(1)}) custom-call(bf16[512,512]{1,0:T(8,128)(2,1)} %outside.1, bf16[512,512]{1,0:T(8,128)(2,1)} %inside_head.1, bf16[512,512]{1,0:T(8,128)(2,1)} %inside_tail.1, f32[512,512]{1,0:T(8,128)} %inside_pair.1, s32[1,512]{1,0:T(1,128)} %seq_head_any.1, s32[1,512]{1,0:T(1,128)} %seq_tail_any.1, ...), custom_call_target="tpu_custom_call" | custom-call | tf_op jit(solution)/shard_map/outside_window/pallas_call | solution.py:499
  26.0 1.3 %put_out.1 = (f32[512,512]{1,0:T(8,128)}, f32[512,512]{1,0:T(8,128)}) custom-call(f32[512,512]{1,0:T(8,128)S(1)} %get-tuple-element.4.diag, f32[512,512]{1,0:T(8,128)S(1)} %get-tuple-element.5.prob), custom_call_target="tpu_custom_call" | custom-call | tf_op jit(solution)/shard_map/put_out/pallas_call | solution.py:537

commit v6 on v5

--- a/solution.py
+++ b/solution.py
@@ -15,7 +15,7 @@
 RIGHT_CHUNK = 32
 RIGHT_CHUNKS = BLK // RIGHT_CHUNK
 SHORT = 5
-LEFT_CHUNK = 64
+LEFT_CHUNK = 128
 LEFT_CHUNKS = BLK // LEFT_CHUNK
 HALF_CHUNKS = LEFT_CHUNKS // 2
 

time: 27.4 us -> 27.2 us (level)
  Pallas kernels: 25.4 us -> 25.1 us
where the time goes in v6:
time: 27.2 us; the launch traced here: 27 us
  Pallas kernels  25.1 us (92%)
  between operations  1.93 us (7%)
    pallas_call x1, Pallas kernels, per_device(): pl.pallas_call(kernel, out_shape=(tile, tile), in_specs=[hbm] * 9 + [smem...  23.8 us
    pallas_call x1, Pallas kernels, per_device(): pl.pallas_call(put_out, out_shape=(tile, tile), in_specs=[vmem] * 2, out_...  1.33 us

profile of v6, /device:TPU:6, one launch (start us, length us, event | category | flops | bytes accessed | tf_op | source)
XLA Modules:
  0.0 27.0 jit_solution(3867414008244817807)
XLA Ops:
  1.9 23.8 %outside_window.1 = (f32[512,512]{1,0:T(8,128)S(1)}, f32[512,512]{1,0:T(8,128)S(1)}) custom-call(bf16[512,512]{1,0:T(8,128)(2,1)} %outside.1, bf16[512,512]{1,0:T(8,128)(2,1)} %inside_head.1, bf16[512,512]{1,0:T(8,128)(2,1)} %inside_tail.1, f32[512,512]{1,0:T(8,128)} %inside_pair.1, s32[1,512]{1,0:T(1,128)} %seq_head_any.1, s32[1,512]{1,0:T(1,128)} %seq_tail_any.1, ...), custom_call_target="tpu_custom_call" | custom-call | tf_op jit(solution)/shard_map/outside_window/pallas_call | solution.py:499
  25.7 1.3 %put_out.1 = (f32[512,512]{1,0:T(8,128)}, f32[512,512]{1,0:T(8,128)}) custom-call(f32[512,512]{1,0:T(8,128)S(1)} %get-tuple-element.4.diag, f32[512,512]{1,0:T(8,128)S(1)} %get-tuple-element.5.prob), custom_call_target="tpu_custom_call" | custom-call | tf_op jit(solution)/shard_map/put_out/pallas_call | solution.py:537
